TPU v7x, 32 devices: a whole 2x2x4 slice. The times are simulated.
32 devices in a mesh: dp: 8 (over z, core), expert: 4 (over y, x).
Axes of the slice: x: 2, y: 2, z: 4, core: 2. Of those that a mesh axis runs over, the one named last changes fastest.
Arguments:
- tokens: bfloat16 [8192, 1024], P(('dp', 'expert')), may hold values from -6 to 6
- router: bfloat16 [1024, 4], replicated, may hold values from -0.1875 to 0.1875
- w_in: bfloat16 [4, 1024, 2048], P('expert'), may hold values from -0.1875 to 0.1875
- w_out: bfloat16 [4, 2048, 1024], P('expert'), may hold values from -0.125 to 0.125
- assign: int32 [8192], P(('dp', 'expert')), may hold values from 0 to 3, as said below
- modality: int32 [8192], P(('dp', 'expert')), may hold values from 0 to 1
- slot: int32 [8192], P(('dp', 'expert')), may hold values from 0 to 95, as said below
Outputs:
- mixed: bfloat16 [8192, 1024], P(('dp', 'expert'))
- importance: float32 [2, 4], replicated
- entropies: float32 [2, 2], replicated
Inputs may be any that keep to these rules, and one draw needn't show every extreme that they name: `assign`: in the rows of one device each expert is named at most 96 times; in every device's rows one expert is named exactly 96 times, the same expert for all devices of one index of dp. A token's slot is the number of earlier rows of the same device that name the same expert.
All inputs are finite; a program needn't handle non-finite values.
Results may differ from a plain program's by a relative error of at most 0.003.
The roundings to bfloat16 on the way count: a program that leaves them out, or rounds other values in their place, can miss the bound.
Values may be sent and summed in bfloat16 or wider, within the bound.
A program may use at most 64 MiB of HBM per device.

v0:
```python
import jax
import jax.numpy as jnp
from jax import lax
from jax.sharding import PartitionSpec as P


def local_statistics(probs, token_entropy, modality):
    kinds = (modality[:, None] == jnp.arange(2, dtype=jnp.int32)[None, :]).astype(jnp.float32)
    sums = jnp.dot(kinds.T, probs, precision=lax.Precision.HIGHEST)
    counts = jnp.sum(kinds, axis=0)
    ent_sum = jnp.dot(kinds.T, token_entropy, precision=lax.Precision.HIGHEST)
    return (sums, counts, ent_sum)


def reduce_statistics(parts):
    grouped = lax.psum((parts[0], parts[1], parts[2]), "expert")
    return lax.psum((grouped[0], grouped[1], grouped[2]), "dp")


def per_device(tokens, router, w_in, w_out, assign, modality, slot):
    logits = jnp.dot(tokens, router, preferred_element_type=jnp.float32)
    probs = jax.nn.softmax(logits, axis=-1)
    logp = jax.nn.log_softmax(logits, axis=-1)
    n_expert = router.shape[1]
    slot_count = 3 * tokens.shape[0] // (2 * n_expert)
    picked = (assign[:, None] == jnp.arange(n_expert, dtype=jnp.int32)[None, :]).astype(jnp.float32)
    gate = jnp.sum(probs * picked, axis=-1)
    token_entropy = -jnp.sum(probs * logp, axis=-1)
    parts = local_statistics(probs, token_entropy, modality)
    labels = assign * slot_count + slot
    placing = (
        labels[None, :] == jnp.arange(n_expert * slot_count, dtype=jnp.int32)[:, None]
    ).astype(jnp.bfloat16)
    buffer = jnp.dot(placing, tokens, preferred_element_type=jnp.float32).astype(jnp.bfloat16)
    buffer = buffer.reshape(n_expert, slot_count, tokens.shape[1])
    first = w_in[0]
    second = w_out[0]
    received = lax.all_to_all(buffer, "expert", split_axis=0, concat_axis=0, tiled=True)
    sources, items, width = received.shape
    rows = received.reshape(sources * items, width)
    hidden = jax.nn.gelu(jnp.dot(rows, first, preferred_element_type=jnp.float32)).astype(
        jnp.bfloat16
    )
    result = jnp.dot(hidden, second, preferred_element_type=jnp.float32).astype(jnp.bfloat16)
    computed = result.reshape(sources, items, width)
    returned = lax.all_to_all(computed, "expert", split_axis=0, concat_axis=0, tiled=True)
    flat = returned.reshape(n_expert * slot_count, tokens.shape[1])
    chosen = jnp.dot(placing.T, flat, preferred_element_type=jnp.float32)
    mixed = (gate[:, None] * chosen).astype(jnp.bfloat16)
    totals = reduce_statistics(parts)
    sums, counts, ent_sum = totals
    denom = jnp.maximum(counts, 1.0)
    importance = sums / denom[:, None]
    global_ent = -jnp.sum(jax.scipy.special.xlogy(importance, importance), axis=-1)
    entropies = jnp.stack([ent_sum / denom, global_ent], axis=1)
    return (mixed, importance, entropies)


def solution(mesh):
    return jax.shard_map(
        per_device,
        mesh=mesh,
        in_specs=(
            P(("dp", "expert"), None),
            P(),
            P("expert", None, None),
            P("expert", None, None),
            P(("dp", "expert")),
            P(("dp", "expert")),
            P(("dp", "expert")),
        ),
        out_specs=(P(("dp", "expert"), None), P(), P()),
        check_vma=False,
    )
```

profile of v0, /device:TPU:0, one launch (start us, length us, event | category | flops | bytes accessed | tf_op | source)
XLA Modules:
  0.0 59.7 jit_solution(12169991942539099799)
XLA Ops:
  0.6 0.0 copy-start
  0.6 0.0 copy-start.1
  0.7 0.0 copy-start.2
  0.7 0.8 %multiply_add_fusion = s32[256]{0:T(256)S(1)} fusion(s32[256]{0:T(256)} %param.13, s32[256]{0:T(256)} %param.11), kind=kLoop, calls=%fused_computation.36 | loop fusion | flops 512 | bytes 3072 | tf_op jit(solution)/shard_map/add | solution.py:30
  1.4 0.3 copy-done
  1.7 1.3 %convolution_convert_fusion = bf16[384,1024]{1,0:T(8,128)(2,1)} fusion(bf16[256,1024]{1,0:T(8,128)(2,1)S(1)} %copy-done, s32[256]{0:T(256)S(1)} %multiply_add_fusion), kind=kOutput, calls=%fused_computation.14 | convolution fusion | flops 201818112 | bytes 1311744 | tf_op jit(solution)/shard_map/dot_general | solution.py:34
  3.0 5.2 %all-to-all-start = ((bf16[4,96,1024]{2,1,0:T(8,128)(2,1)}), bf16[4,96,1024]{2,1,0:T(8,128)(2,1)S(1)}, u32[]{:S(2)}, u32[]{:S(2)}) async-start(bf16[4,96,1024]{2,1,0:T(8,128)(2,1)} %bitcast), calls=%async_computation | async-start | bytes 1572864 | tf_op jit(solution)/shard_map/all_to_all | solution.py:38
  8.1 1.0 %fusion.32 = (f32[256]{0:T(256)S(1)}, f32[256,4]{0,1:T(4,128)S(1)}) fusion(bf16[256,1024]{1,0:T(8,128)(2,1)S(1)} %copy-done, bf16[1024,4]{0,1:T(4,128)(2,1)} %param.8), kind=kOutput, calls=%fused_computation.46 | convolution fusion | flops 2097920 | bytes 537600 | tf_op jit(solution)/shard_map/dot_general | solution.py:21
  9.1 0.0 copy-done.1
  9.2 0.0 copy-done.2
  9.2 0.1 convolution_bitcast_fusion
  9.3 0.1 fusion.24
  9.4 0.1 convert_reduce_fusion
  9.6 12.6 %all-reduce.1 = (f32[2,4]{1,0:T(2,128)S(1)}, f32[2]{0:T(128)S(1)}, f32[2]{0:T(128)S(1)}) all-reduce(f32[2,4]{1,0:T(2,128)S(1)} %fusion.24, f32[2]{0:T(128)S(1)} %convert_reduce_fusion, f32[2]{0:T(128)S(1)} %convolution_bitcast_fusion), channel_id=1, replica_groups=mesh['dp'=8,'expert'=4] {'expert'}, use_global_device_ids=true, to_apply=%region_3.0 | all-reduce | flops 12 | bytes 96 | tf_op jit(solution)/shard_map/psum | solution.py:16
  22.1 14.8 %all-reduce = (f32[2,4]{1,0:T(2,128)S(1)}, f32[2]{0:T(128)S(1)}, f32[2]{0:T(128)S(1)}) all-reduce(f32[2,4]{1,0:T(2,128)S(1)} %get-tuple-element.14, f32[2]{0:T(128)S(1)} %get-tuple-element.15, f32[2]{0:T(128)S(1)} %get-tuple-element.16), channel_id=1, replica_groups=mesh['dp'=8,'expert'=4] {'dp'}, use_global_device_ids=true, to_apply=%region_4.5 | all-reduce | flops 12 | bytes 96 | tf_op jit(solution)/shard_map/psum | solution.py:17
  36.9 0.0 all-to-all-done
  36.9 7.9 %fusion.14 = bf16[384,1024]{1,0:T(8,128)(2,1)} fusion(bf16[1,2048,1024]{2,1,0:T(8,128)(2,1)} %param.10, bf16[384,1024]{1,0:T(8,128)(2,1)S(1)} %bitcast.30, bf16[1,1024,2048]{2,1,0:T(8,128)(2,1)} %param.9), kind=kOutput, calls=%fused_computation.13 | convolution fusion | flops 3228696576 | bytes 9961472 | tf_op jit(solution)/shard_map/dot_general | solution.py:44
  44.9 3.5 %all-to-all-start.1 = ((bf16[4,96,1024]{2,1,0:T(8,128)(2,1)}), bf16[4,96,1024]{2,1,0:T(8,128)(2,1)S(1)}, u32[]{:S(2)}, u32[]{:S(2)}) async-start(bf16[4,96,1024]{2,1,0:T(8,128)(2,1)} %bitcast.4), calls=%async_computation.1 | async-start | bytes 1572864 | tf_op jit(solution)/shard_map/all_to_all | solution.py:46
  48.4 0.7 %fusion.27 = (f32[2]{0:T(128)S(1)}, f32[2,4]{1,0:T(2,128)}) fusion(f32[2,4]{1,0:T(2,128)S(1)} %get-tuple-element.11, f32[2]{0:T(128)S(1)} %get-tuple-element.21), kind=kLoop, calls=%fused_computation.37 | loop fusion | flops 54 | bytes 80 | tf_op jit(solution)/shard_map/reduce_sum | solution.py:54
  49.2 0.7 %copy.11 = f32[2,2]{1,0:T(2,128)} copy(f32[2,2]{0,1:T(2,128)S(1)} %pad_maximum_fusion) | data formatting | bytes 32
  49.8 8.6 %all-to-all-done.1 = bf16[4,96,1024]{2,1,0:T(8,128)(2,1)S(1)} async-done(((bf16[4,96,1024]{2,1,0:T(8,128)(2,1)}), bf16[4,96,1024]{2,1,0:T(8,128)(2,1)S(1)}, u32[]{:S(2)}, u32[]{:S(2)}) %all-to-all-start.1) | async-done | bytes 786464 | tf_op jit(solution)/shard_map/all_to_all | solution.py:46
  58.4 1.3 %fusion.17 = bf16[256,1024]{1,0:T(8,128)(2,1)} fusion(bf16[384,1024]{1,0:T(8,128)(2,1)S(1)} %bitcast.31, f32[256]{0:T(256)S(1)} %get-tuple-element.10, s32[256]{0:T(256)S(1)} %multiply_add_fusion), kind=kOutput, calls=%fused_computation.16 | convolution fusion | flops 201949184 | bytes 1312768 | tf_op jit(solution)/shard_map/dot_general | solution.py:48
  (7 shorter events, 0.1 us)
Async XLA Ops:
  0.6 1.1 %copy-start = (bf16[256,1024]{1,0:T(8,128)(2,1)S(1)}, bf16[256,1024]{1,0:T(8,128)(2,1)}, u32[]{:S(2)}) copy-start(bf16[256,1024]{1,0:T(8,128)(2,1)} %param.7) | copy-start | bytes 1572868
  0.6 8.5 %copy-start.1 = (s32[256]{0:T(256)S(1)}, s32[256]{0:T(256)}, u32[]{:S(2)}) copy-start(s32[256]{0:T(256)} %param.11) | copy-start | bytes 3076
  0.7 8.5 %copy-start.2 = (s32[256]{0:T(256)S(1)}, s32[256]{0:T(256)}, u32[]{:S(2)}) copy-start(s32[256]{0:T(256)} %param.12) | copy-start | bytes 3076
  3.0 34.0 %all-to-all-start = ((bf16[4,96,1024]{2,1,0:T(8,128)(2,1)}), bf16[4,96,1024]{2,1,0:T(8,128)(2,1)S(1)}, u32[]{:S(2)}, u32[]{:S(2)}) async-start(bf16[4,96,1024]{2,1,0:T(8,128)(2,1)} %bitcast), calls=%async_computation | async-start | bytes 1572864 | tf_op jit(solution)/shard_map/all_to_all | solution.py:38
  44.9 13.6 %all-to-all-start.1 = ((bf16[4,96,1024]{2,1,0:T(8,128)(2,1)}), bf16[4,96,1024]{2,1,0:T(8,128)(2,1)S(1)}, u32[]{:S(2)}, u32[]{:S(2)}) async-start(bf16[4,96,1024]{2,1,0:T(8,128)(2,1)} %bitcast.4), calls=%async_computation.1 | async-start | bytes 1572864 | tf_op jit(solution)/shard_map/all_to_all | solution.py:46
where the time goes:
time: 60.1 us; the launch traced here: 59.7 us
  blocking collectives  27.4 us (46%)
  matrix products  11.7 us (19%)
  starting transfers between devices  8.65 us (14%)
  waiting for transfers between devices  8.62 us (14%)
  other arithmetic  1.7 us (3%)
  local copies, waits for them, and re-layouts  0.96 us (2%)
  between operations  0.73 us (1%)
    psum x1, blocking collectives, reduce_statistics(): return lax.psum((grouped[0], grouped[1], grouped[2]), 'dp')  14.8 us
    psum x1, blocking collectives, reduce_statistics(): grouped = lax.psum((parts[0], parts[1], parts[2]), 'expert')  12.6 us
    all_to_all x1, waiting for transfers between devices, per_device(): lax.all_to_all(computed, 'expert', split_axis=0, concat_axis=0, tiled=True)  8.62 us
    dot_general x1, matrix products, per_device(): jnp.dot(hidden, second, preferred_element_type=jnp.float32)  7.93 us
    all_to_all x1, starting transfers between devices, per_device(): lax.all_to_all(buffer, 'expert', split_axis=0, concat_axis=0, tiled=True)  5.16 us
    all_to_all x1, starting transfers between devices, per_device(): lax.all_to_all(computed, 'expert', split_axis=0, concat_axis=0, tiled=True)  3.49 us
    dot_general x1, matrix products, per_device(): chosen = jnp.dot(placing.T, flat, preferred_element_type=jnp.float32)  1.29 us
    dot_general x1, matrix products, per_device(): jnp.dot(placing, tokens, preferred_element_type=jnp.float32)  1.25 us
  transfers between devices with their start and end apart: 2, of which 1 were waited for; matrix products, arithmetic and copies ran while one was open for 5% of the time, Pallas kernels for 0%

commit v1 on v0

v1 whole, which is shorter than its diff:
```python
import functools

import jax
import jax.numpy as jnp
from jax import lax
from jax.experimental import pallas as pl
from jax.experimental.pallas import tpu as pltpu
from jax.sharding import PartitionSpec as P

MESH = pl.DeviceIdType.MESH


def partner(me, k, n):
    out, bit = 0, 1
    while bit < n:
        digit = lax.rem(lax.div(me, bit), 2)
        if k & bit:
            digit = 1 - digit
        out = out + digit * bit
        bit *= 2
    return out


def to_columns(row):
    return jnp.transpose(jnp.broadcast_to(row, (128, row.shape[1])))


def kernel(
    n, n_dp, cap, chunks, tokens_hbm, router_t, w_in_hbm, w_out_hbm, assign, modality, slot,
    mixed, importance, entropies,
    tokens, w1, w2, buf, recv, res, ret, hidden, chosen, stat1, stat2,
    tok_sem, w1_sem, w2_sem, out_send, out_recv, back_send, back_recv, s1_send, s1_recv, s2_send, s2_recv,
):
    me = lax.axis_index("expert")
    me_dp = lax.axis_index("dp")
    peers = [partner(me, k, n) for k in range(n)]
    peers_dp = [partner(me_dp, k, n_dp) for k in range(n_dp)]
    n_tok, width = tokens.shape
    n_exp = router_t.shape[0]
    part = cap // chunks
    span = (n - 1) * part

    tok_copy = pltpu.make_async_copy(tokens_hbm, tokens, tok_sem)
    tok_copy.start()
    barrier = pltpu.get_barrier_semaphore()
    for k in range(1, n):
        pl.semaphore_signal(barrier, inc=1, device_id={"expert": peers[k]}, device_id_type=MESH)
    for k in range(1, n_dp):
        pl.semaphore_signal(barrier, inc=1, device_id={"dp": peers_dp[k]}, device_id_type=MESH)

    n1, n2 = w1.shape[0], w2.shape[0]
    c1, c2 = w1.shape[2], w2.shape[2]

    def w1_copy(j):
        return pltpu.make_async_copy(w_in_hbm.at[0, :, pl.ds(j * c1, c1)], w1.at[j], w1_sem.at[j])

    def w2_copy(j):
        return pltpu.make_async_copy(w_out_hbm.at[0, :, pl.ds(j * c2, c2)], w2.at[j], w2_sem.at[j])

    rel = jnp.bitwise_xor(assign[...], me)
    where_slot = slot[...]
    piece = lax.div(where_slot, part)
    label = jnp.where(
        rel == 0, where_slot, cap + piece * span + (rel - 1) * part + where_slot - piece * part
    )

    def place(start, count):
        rows = lax.broadcasted_iota(jnp.int32, (count, n_tok), 0) + start
        one_hot = jnp.where(rows == label, 1.0, 0.0).astype(jnp.bfloat16)
        buf[start : start + count, :] = jnp.dot(
            one_hot, tokens[...], preferred_element_type=jnp.float32
        ).astype(jnp.bfloat16)

    def rows_of(c, k):
        return pl.ds(cap + c * span + (k - 1) * part, part)

    def send(src, dst, sems, c, k):
        rows = rows_of(c, k)
        return pltpu.make_async_remote_copy(
            src_ref=src.at[rows], dst_ref=dst.at[rows],
            send_sem=sems[0].at[c, k], recv_sem=sems[1].at[c, k],
            device_id={"expert": peers[k]}, device_id_type=MESH,
        )

    def out_copy(c, k):
        return send(buf, recv, (out_send, out_recv), c, k)

    def back_copy(c, k):
        return send(res, ret, (back_send, back_recv), c, k)

    tok_copy.wait()
    for j in range(n1):
        w1_copy(j).start()
    for j in range(n2):
        w2_copy(j).start()
    for c in range(chunks):
        place(cap + c * span, span)
        if c == 0:
            pl.semaphore_wait(barrier, n - 1 + n_dp - 1)
        for k in reversed(range(1, n)):
            out_copy(c, k).start()
    place(0, cap)

    logits = lax.dot_general(
        router_t[...], tokens[...], (((1,), (1,)), ((), ())), preferred_element_type=jnp.float32
    )
    shifted = logits - jnp.max(logits, axis=0, keepdims=True)
    unnorm = jnp.exp(shifted)
    total = jnp.sum(unnorm, axis=0, keepdims=True)
    probs = unnorm / total
    logp = shifted - jnp.log(total)
    picked = lax.broadcasted_iota(jnp.int32, probs.shape, 0) == assign[...]
    gate = jnp.sum(jnp.where(picked, probs, 0.0), axis=0, keepdims=True)
    entropy = -jnp.sum(probs * logp, axis=0, keepdims=True)
    kinds = [(modality[...] == m).astype(jnp.float32) for m in range(2)]

    def by_kind(values):
        first, second = (jnp.sum(values * kind, axis=1, keepdims=True) for kind in kinds)
        lane = lax.broadcasted_iota(jnp.int32, (values.shape[0], 128), 1)
        return jnp.where(lane == 0, first, jnp.where(lane == 1, second, 0.0))

    stat1[me] = jnp.zeros(stat1.shape[1:], jnp.float32)
    stat1[me, 0:n_exp, :] = by_kind(probs)
    stat1[me, n_exp : n_exp + 1, :] = by_kind(jnp.ones_like(gate))
    stat1[me, n_exp + 1 : n_exp + 2, :] = by_kind(entropy)

    def s1_copy(k):
        return pltpu.make_async_remote_copy(
            src_ref=stat1.at[me], dst_ref=stat1.at[me], send_sem=s1_send.at[k],
            recv_sem=s1_recv.at[k], device_id={"expert": peers[k]}, device_id_type=MESH,
        )

    def s2_copy(k):
        return pltpu.make_async_remote_copy(
            src_ref=stat2.at[me_dp], dst_ref=stat2.at[me_dp], send_sem=s2_send.at[k],
            recv_sem=s2_recv.at[k], device_id={"dp": peers_dp[k]}, device_id_type=MESH,
        )

    for k in range(1, n):
        s1_copy(k).start()

    def experts(src, dst, start, count, first):
        @pl.loop(0, n1)
        def _(j):
            if first:
                w1_copy(j).wait()
            act = jax.nn.gelu(
                jnp.dot(src[start : start + count, :], w1[j], preferred_element_type=jnp.float32)
            )
            hidden[0:count, pl.ds(pl.multiple_of(j * c1, c1), c1)] = act.astype(jnp.bfloat16)

        @pl.loop(0, n2)
        def _(j):
            if first:
                w2_copy(j).wait()
            dst[start : start + count, pl.ds(pl.multiple_of(j * c2, c2), c2)] = jnp.dot(
                hidden[0:count, :], w2[j], preferred_element_type=jnp.float32
            ).astype(jnp.bfloat16)

    experts(buf, ret, 0, cap, True)

    for k in range(1, n):
        s1_copy(k).wait()
    stat2[me_dp] = sum(stat1[i] for i in range(n))
    for k in range(1, n_dp):
        s2_copy(k).start()

    for c in range(chunks):
        for k in range(1, n):
            out_copy(c, k).wait_recv()
        experts(recv, res, cap + c * span, span, False)
        for k in reversed(range(1, n)):
            back_copy(c, k).start()

    label_columns = to_columns(label.astype(jnp.float32))
    gate_column = to_columns(gate)[:, 0:1]

    def gather(start, count):
        lanes = lax.broadcasted_iota(jnp.int32, (n_tok, count), 1) + start
        one_hot = jnp.where(lanes.astype(jnp.float32) == label_columns[:, 0:1], 1.0, 0.0)
        return jnp.dot(
            one_hot.astype(jnp.bfloat16), ret[start : start + count, :],
            preferred_element_type=jnp.float32,
        )

    chosen[...] = gather(0, cap)

    for k in range(1, n_dp):
        s2_copy(k).wait()
    totals = jnp.transpose(sum(stat2[i] for i in range(n_dp)))
    denom = jnp.maximum(totals[0:2, n_exp : n_exp + 1], 1.0)
    mean = totals[0:2, 0:n_exp] / denom
    importance[...] = mean
    logs = jnp.log(jnp.where(mean == 0.0, 1.0, mean))
    entropies[:, 0:1] = totals[0:2, n_exp + 1 : n_exp + 2] / denom
    entropies[:, 1:2] = -jnp.sum(mean * logs, axis=1, keepdims=True)

    for c in range(chunks):
        for k in range(1, n):
            back_copy(c, k).wait_recv()
        if c < chunks - 1:
            chosen[...] += gather(cap + c * span, span)
        else:
            mixed[...] = (
                gate_column * (chosen[...] + gather(cap + c * span, span))
            ).astype(jnp.bfloat16)

    for c in range(chunks):
        for k in range(1, n):
            out_copy(c, k).wait_send()
            back_copy(c, k).wait_send()


def per_device(n, n_dp, tokens, router, w_in, w_out, assign, modality, slot):
    n_tok, width = tokens.shape
    n_exp = router.shape[1]
    ff = w_in.shape[2]
    cap = -(-(3 * n_tok // (2 * n_exp)) // 16) * 16
    chunks = 2 if cap % 32 == 0 else 1
    rows = n * cap
    c1, c2 = min(ff, 512), min(width, 256)
    stat_rows = -(-(n_exp + 2) // 8) * 8
    vmem = pl.BlockSpec(memory_space=pltpu.VMEM)
    hbm = pl.BlockSpec(memory_space=pl.ANY)
    dma = pltpu.SemaphoreType.DMA
    block = pltpu.VMEM((rows, width), jnp.bfloat16)
    return pl.pallas_call(
        functools.partial(kernel, n, n_dp, cap, chunks),
        out_shape=(
            jax.ShapeDtypeStruct((n_tok, width), jnp.bfloat16),
            jax.ShapeDtypeStruct((2, n_exp), jnp.float32),
            jax.ShapeDtypeStruct((2, 2), jnp.float32),
        ),
        in_specs=[hbm, vmem, hbm, hbm, vmem, vmem, vmem],
        out_specs=(vmem, vmem, vmem),
        scratch_shapes=[
            pltpu.VMEM((n_tok, width), jnp.bfloat16),
            pltpu.VMEM((ff // c1, width, c1), jnp.bfloat16),
            pltpu.VMEM((width // c2, ff, c2), jnp.bfloat16),
            block, block, block, block,
            pltpu.VMEM((max(cap, rows - cap), ff), jnp.bfloat16),
            pltpu.VMEM((n_tok, width), jnp.float32),
            pltpu.VMEM((n, stat_rows, 128), jnp.float32),
            pltpu.VMEM((n_dp, stat_rows, 128), jnp.float32),
            dma, dma((ff // c1,)), dma((width // c2,)),
            dma((chunks, n)), dma((chunks, n)), dma((chunks, n)), dma((chunks, n)),
            dma((n,)), dma((n,)), dma((n_dp,)), dma((n_dp,)),
        ],
        compiler_params=pltpu.CompilerParams(
            collective_id=0, has_side_effects=True, vmem_limit_bytes=40 * 2**20
        ),
        cost_estimate=pl.CostEstimate(
            flops=4 * rows * width * ff, bytes_accessed=4 * width * ff, transcendentals=rows * ff
        ),
    )(
        tokens, router.T, w_in, w_out,
        assign.reshape(1, n_tok), modality.reshape(1, n_tok), slot.reshape(1, n_tok),
    )


def solution(mesh):
    return jax.shard_map(
        functools.partial(per_device, mesh.shape["expert"], mesh.shape["dp"]),
        mesh=mesh,
        in_specs=(
            P(("dp", "expert"), None),
            P(),
            P("expert", None, None),
            P("expert", None, None),
            P(("dp", "expert")),
            P(("dp", "expert")),
            P(("dp", "expert")),
        ),
        out_specs=(P(("dp", "expert"), None), P(), P()),
        check_vma=False,
    )
```

time: 60.1 us -> 41.9 us (0.70)
  Pallas kernels: 0 us -> 30.9 us
  blocking collectives: 27.4 us -> 0 us
  matrix products: 11.7 us -> 0 us
  local copies, waits for them, and re-layouts: 0.96 us -> 10.1 us
  starting transfers between devices: 8.65 us -> 0 us
  waiting for transfers between devices: 8.62 us -> 0 us
  other arithmetic: 1.7 us -> 0 us
    pallas_call x0 -> x1, Pallas kernels: none -> 30.9 us  [per_device(): pl.pallas_call(functools.partial(kernel, n, n_dp, cap, chunks), out_shape...]
    psum x2 -> x0, blocking collectives: 27.4 us -> none  [the longest x1 14.8 us: reduce_statistics(): return lax.psum((grouped[0], grouped[1], grouped[2]), 'dp')]
    dot_general x6 -> x0, matrix products: 11.7 us -> none  [the longest x1 7.93 us: per_device(): jnp.dot(hidden, second, preferred_element_type=jnp.float32)]
    unnamed x7 -> x17, local copies, waits for them, and re-layouts: 0.96 us -> 10.1 us
    all_to_all x2 -> x0, starting transfers between devices: 8.65 us -> none  [the longest x1 5.16 us: per_device(): lax.all_to_all(buffer, 'expert', split_axis=0, concat_axis=0, tiled=True)]
    all_to_all x2 -> x0, waiting for transfers between devices: 8.62 us -> none  [the longest x1 8.62 us: per_device(): lax.all_to_all(computed, 'expert', split_axis=0, concat_axis=0, tiled=True)]
    reduce_sum x4 -> x0, other arithmetic: 0.92 us -> none  [the longest x1 0.75 us: per_device(): jnp.sum(jax.scipy.special.xlogy(importance, importance), axis=-1)]
    add x1 -> x0, other arithmetic: 0.75 us -> none  [per_device(): labels = assign * slot_count + slot]
  transfers between devices with their start and end apart: 2 -> 0, of which waited for: 1 -> 0; matrix products, arithmetic and copies ran while one was open for 5% -> 0% of each run, Pallas kernels for 0% -> 0%
where the time goes in v1:
time: 41.9 us; the launch traced here: 41.6 us
  Pallas kernels  30.9 us (74%)
  local copies, waits for them, and re-layouts  10.1 us (24%)
  between operations  0.66 us (2%)
    pallas_call x1, Pallas kernels, per_device(): pl.pallas_call(functools.partial(kernel, n, n_dp, cap, chunks), out_shape...  30.9 us
    unnamed x17, local copies, waits for them, and re-layouts  10.1 us

profile of v1, /device:TPU:0, one launch (start us, length us, event | category | flops | bytes accessed | tf_op | source)
XLA Modules:
  0.0 41.6 jit_solution(7379865253113180745)
XLA Ops:
  0.6 0.0 copy-start
  0.6 2.2 %copy-done = bf16[1,1024,2048]{2,1,0:T(8,128)(2,1)S(1)} copy-done((bf16[1,1024,2048]{2,1,0:T(8,128)(2,1)S(1)}, bf16[1,1024,2048]{2,1,0:T(8,128)(2,1)}, u32[]{:S(2)}) %copy-start) | copy-done | bytes 4194328
  2.8 0.0 copy-start.1
  2.8 2.2 %copy-done.1 = bf16[1,2048,1024]{2,1,0:T(8,128)(2,1)S(1)} copy-done((bf16[1,2048,1024]{2,1,0:T(8,128)(2,1)S(1)}, bf16[1,2048,1024]{2,1,0:T(8,128)(2,1)}, u32[]{:S(2)}) %copy-start.1) | copy-done | bytes 4194328
  5.0 0.0 copy-start.2
  5.0 1.0 %copy-done.2 = bf16[256,1024]{1,0:T(8,128)(2,1)S(1)} copy-done((bf16[256,1024]{1,0:T(8,128)(2,1)S(1)}, bf16[256,1024]{1,0:T(8,128)(2,1)}, u32[]{:S(2)}) %copy-start.2) | copy-done | bytes 524312
  6.1 0.0 copy-start.3
  6.1 0.7 %copy-done.3 = bf16[1024,4]{0,1:T(4,128)(2,1)S(1)} copy-done((bf16[1024,4]{0,1:T(4,128)(2,1)S(1)}, bf16[1024,4]{0,1:T(4,128)(2,1)}, u32[]{:S(2)}) %copy-start.3) | copy-done | bytes 8216
  6.7 0.0 copy-start.4
  6.8 0.7 %copy-done.4 = s32[256]{0:T(256)S(1)} copy-done((s32[256]{0:T(256)S(1)}, s32[256]{0:T(256)}, u32[]{:S(2)}) %copy-start.4) | copy-done | bytes 1048
  7.4 0.0 copy-start.5
  7.4 0.7 %copy-done.5 = s32[256]{0:T(256)S(1)} copy-done((s32[256]{0:T(256)S(1)}, s32[256]{0:T(256)}, u32[]{:S(2)}) %copy-start.5) | copy-done | bytes 1048
  8.1 0.0 copy-start.6
  8.1 0.7 %copy-done.6 = s32[256]{0:T(256)S(1)} copy-done((s32[256]{0:T(256)S(1)}, s32[256]{0:T(256)}, u32[]{:S(2)}) %copy-start.6) | copy-done | bytes 1048
  8.8 30.9 %shard_map.94 = (bf16[256,1024]{1,0:T(8,128)(2,1)S(1)}, f32[2,4]{1,0:T(2,128)S(1)}, f32[2,2]{1,0:T(2,128)S(1)}) custom-call(bf16[256,1024]{1,0:T(8,128)(2,1)S(1)} %copy-done.2, bf16[4,1024]{1,0:T(4,128)(2,1)S(1)} %bitcast.4, bf16[1,1024,2048]{2,1,0:T(8,128)(2,1)S(1)} %copy-done, bf16[1,2048,1024]{2,1,0:T(8,128)(2,1)S(1)} %copy-done.1, s32[1,256]{1,0:T(1,128)S(1)} %bitcast.5, ...), custom_call_target="tpu_custom_call" | custom-call | flops 3221225472 | bytes 8388608 | tf_op jit(solution)/shard_map/pallas_call | solution.py:227
  39.7 0.8 %copy.13 = bf16[256,1024]{1,0:T(8,128)(2,1)} copy(bf16[256,1024]{1,0:T(8,128)(2,1)S(1)} %get-tuple-element.6) | data formatting | bytes 1048576
  40.5 0.6 %copy.14 = f32[2,4]{1,0:T(2,128)} copy(f32[2,4]{1,0:T(2,128)S(1)} %get-tuple-element.7) | data formatting | bytes 64
  41.0 0.6 %copy.15 = f32[2,2]{1,0:T(2,128)} copy(f32[2,2]{1,0:T(2,128)S(1)} %get-tuple-element.8) | data formatting | bytes 32
Async XLA Ops:
  0.6 2.2 %copy-start = (bf16[1,1024,2048]{2,1,0:T(8,128)(2,1)S(1)}, bf16[1,1024,2048]{2,1,0:T(8,128)(2,1)}, u32[]{:S(2)}) copy-start(bf16[1,1024,2048]{2,1,0:T(8,128)(2,1)} %w_in_hbm.1) | copy-start | bytes 12582916
  2.8 2.2 %copy-start.1 = (bf16[1,2048,1024]{2,1,0:T(8,128)(2,1)S(1)}, bf16[1,2048,1024]{2,1,0:T(8,128)(2,1)}, u32[]{:S(2)}) copy-start(bf16[1,2048,1024]{2,1,0:T(8,128)(2,1)} %w_out_hbm.1) | copy-start | bytes 12582916
  5.0 1.0 %copy-start.2 = (bf16[256,1024]{1,0:T(8,128)(2,1)S(1)}, bf16[256,1024]{1,0:T(8,128)(2,1)}, u32[]{:S(2)}) copy-start(bf16[256,1024]{1,0:T(8,128)(2,1)} %tokens_hbm.1) | copy-start | bytes 1572868
  6.1 0.7 %copy-start.3 = (bf16[1024,4]{0,1:T(4,128)(2,1)S(1)}, bf16[1024,4]{0,1:T(4,128)(2,1)}, u32[]{:S(2)}) copy-start(bf16[1024,4]{0,1:T(4,128)(2,1)} %param.8) | copy-start | bytes 24580
  6.7 0.7 %copy-start.4 = (s32[256]{0:T(256)S(1)}, s32[256]{0:T(256)}, u32[]{:S(2)}) copy-start(s32[256]{0:T(256)} %param.11) | copy-start | bytes 3076
  7.4 0.7 %copy-start.5 = (s32[256]{0:T(256)S(1)}, s32[256]{0:T(256)}, u32[]{:S(2)}) copy-start(s32[256]{0:T(256)} %param.12) | copy-start | bytes 3076
  8.1 0.7 %copy-start.6 = (s32[256]{0:T(256)S(1)}, s32[256]{0:T(256)}, u32[]{:S(2)}) copy-start(s32[256]{0:T(256)} %param.13) | copy-start | bytes 3076

commit v2 on v1

--- a/solution.py
+++ b/solution.py
@@ -8,6 +8,7 @@
 from jax.sharding import PartitionSpec as P
 
 MESH = pl.DeviceIdType.MESH
+VMEM_LIMIT = 63 * 2**20
 
 
 def partner(me, k, n):
@@ -26,10 +27,11 @@
 
 
 def kernel(
-    n, n_dp, cap, chunks, tokens_hbm, router_t, w_in_hbm, w_out_hbm, assign, modality, slot,
-    mixed, importance, entropies,
-    tokens, w1, w2, buf, recv, res, ret, hidden, chosen, stat1, stat2,
-    tok_sem, w1_sem, w2_sem, out_send, out_recv, back_send, back_recv, s1_send, s1_recv, s2_send, s2_recv,
+    n, n_dp, cap, chunks,
+    tokens_hbm, router_hbm, w_in_hbm, w_out_hbm, assign_hbm, modality_hbm, slot_hbm,
+    mixed_hbm, importance_hbm, entropies_hbm,
+    mixed, importance, entropies, tokens, router_t, assign, modality, slot, w1, w2, buf, recv, res, ret, hidden, chosen, stat1, stat2,
+    in_sem, out_sem, w1_sem, w2_sem, out_send, out_recv, back_send, back_recv, s1_send, s1_recv, s2_send, s2_recv,
 ):
     me = lax.axis_index("expert")
     me_dp = lax.axis_index("dp")
@@ -40,8 +42,13 @@
     part = cap // chunks
     span = (n - 1) * part
 
-    tok_copy = pltpu.make_async_copy(tokens_hbm, tokens, tok_sem)
-    tok_copy.start()
+    pairs = (
+        (assign_hbm, assign), (slot_hbm, slot), (tokens_hbm, tokens),
+        (router_hbm, router_t), (modality_hbm, modality),
+    )
+    loads = [pltpu.make_async_copy(a, b, in_sem.at[i]) for i, (a, b) in enumerate(pairs)]
+    for load in loads:
+        load.start()
     barrier = pltpu.get_barrier_semaphore()
     for k in range(1, n):
         pl.semaphore_signal(barrier, inc=1, device_id={"expert": peers[k]}, device_id_type=MESH)
@@ -57,6 +64,8 @@
     def w2_copy(j):
         return pltpu.make_async_copy(w_out_hbm.at[0, :, pl.ds(j * c2, c2)], w2.at[j], w2_sem.at[j])
 
+    loads[0].wait()
+    loads[1].wait()
     rel = jnp.bitwise_xor(assign[...], me)
     where_slot = slot[...]
     piece = lax.div(where_slot, part)
@@ -88,7 +97,7 @@
     def back_copy(c, k):
         return send(res, ret, (back_send, back_recv), c, k)
 
-    tok_copy.wait()
+    loads[2].wait()
     for j in range(n1):
         w1_copy(j).start()
     for j in range(n2):
@@ -101,6 +110,8 @@
             out_copy(c, k).start()
     place(0, cap)
 
+    loads[3].wait()
+    loads[4].wait()
     logits = lax.dot_general(
         router_t[...], tokens[...], (((1,), (1,)), ((), ())), preferred_element_type=jnp.float32
     )
@@ -140,20 +151,18 @@
         s1_copy(k).start()
 
     def experts(src, dst, start, count, first):
-        @pl.loop(0, n1)
-        def _(j):
+        for j in range(n1):
             if first:
                 w1_copy(j).wait()
             act = jax.nn.gelu(
                 jnp.dot(src[start : start + count, :], w1[j], preferred_element_type=jnp.float32)
             )
-            hidden[0:count, pl.ds(pl.multiple_of(j * c1, c1), c1)] = act.astype(jnp.bfloat16)
-
-        @pl.loop(0, n2)
-        def _(j):
+            hidden[0:count, pl.ds(j * c1, c1)] = act.astype(jnp.bfloat16)
+
+        for j in range(n2):
             if first:
                 w2_copy(j).wait()
-            dst[start : start + count, pl.ds(pl.multiple_of(j * c2, c2), c2)] = jnp.dot(
+            dst[start : start + count, pl.ds(j * c2, c2)] = jnp.dot(
                 hidden[0:count, :], w2[j], preferred_element_type=jnp.float32
             ).astype(jnp.bfloat16)
 
@@ -175,9 +184,10 @@
     label_columns = to_columns(label.astype(jnp.float32))
     gate_column = to_columns(gate)[:, 0:1]
 
-    def gather(start, count):
-        lanes = lax.broadcasted_iota(jnp.int32, (n_tok, count), 1) + start
-        one_hot = jnp.where(lanes.astype(jnp.float32) == label_columns[:, 0:1], 1.0, 0.0)
+    def gather(start, count, first=0, length=n_tok):
+        lanes = lax.broadcasted_iota(jnp.int32, (length, count), 1) + start
+        wanted = label_columns[first : first + length, 0:1]
+        one_hot = jnp.where(lanes.astype(jnp.float32) == wanted, 1.0, 0.0)
         return jnp.dot(
             one_hot.astype(jnp.bfloat16), ret[start : start + count, :],
             preferred_element_type=jnp.float32,
@@ -195,20 +205,45 @@
     entropies[:, 0:1] = totals[0:2, n_exp + 1 : n_exp + 2] / denom
     entropies[:, 1:2] = -jnp.sum(mean * logs, axis=1, keepdims=True)
 
+    stores = [
+        pltpu.make_async_copy(importance, importance_hbm, out_sem.at[0]),
+        pltpu.make_async_copy(entropies, entropies_hbm, out_sem.at[1]),
+    ]
+    for store in stores:
+        store.start()
+
     for c in range(chunks):
         for k in range(1, n):
             back_copy(c, k).wait_recv()
         if c < chunks - 1:
             chosen[...] += gather(cap + c * span, span)
-        else:
-            mixed[...] = (
-                gate_column * (chosen[...] + gather(cap + c * span, span))
-            ).astype(jnp.bfloat16)
+    half = n_tok // 2
+    for i in range(2):
+        rows = pl.ds(i * half, half)
+        last = gather(cap + (chunks - 1) * span, span, i * half, half)
+        mixed[rows, :] = (
+            gate_column[i * half : (i + 1) * half] * (chosen[rows, :] + last)
+        ).astype(jnp.bfloat16)
+        stores.append(
+            pltpu.make_async_copy(mixed.at[rows], mixed_hbm.at[rows], out_sem.at[2 + i])
+        )
+        stores[-1].start()
+    for store in stores:
+        store.wait()
 
     for c in range(chunks):
         for k in range(1, n):
             out_copy(c, k).wait_send()
             back_copy(c, k).wait_send()
+
+
+def write_out(*refs):
+    sems, count = refs[-1], (len(refs) - 1) // 2
+    copies = [pltpu.make_async_copy(refs[i], refs[count + i], sems.at[i]) for i in range(count)]
+    for copy in copies:
+        copy.start()
+    for copy in copies:
+        copy.wait()
 
 
 def per_device(n, n_dp, tokens, router, w_in, w_out, assign, modality, slot):
@@ -220,21 +255,26 @@
     rows = n * cap
     c1, c2 = min(ff, 512), min(width, 256)
     stat_rows = -(-(n_exp + 2) // 8) * 8
-    vmem = pl.BlockSpec(memory_space=pltpu.VMEM)
-    hbm = pl.BlockSpec(memory_space=pl.ANY)
+    hbm = pl.BlockSpec(memory_space=pltpu.HBM)
     dma = pltpu.SemaphoreType.DMA
     block = pltpu.VMEM((rows, width), jnp.bfloat16)
-    return pl.pallas_call(
+    out_shape = (
+        jax.ShapeDtypeStruct((n_tok, width), jnp.bfloat16),
+        jax.ShapeDtypeStruct((2, n_exp), jnp.float32),
+        jax.ShapeDtypeStruct((2, 2), jnp.float32),
+    )
+    results = pl.pallas_call(
         functools.partial(kernel, n, n_dp, cap, chunks),
-        out_shape=(
-            jax.ShapeDtypeStruct((n_tok, width), jnp.bfloat16),
-            jax.ShapeDtypeStruct((2, n_exp), jnp.float32),
-            jax.ShapeDtypeStruct((2, 2), jnp.float32),
-        ),
-        in_specs=[hbm, vmem, hbm, hbm, vmem, vmem, vmem],
-        out_specs=(vmem, vmem, vmem),
+        out_shape=out_shape,
+        in_specs=[hbm] * 7,
+        out_specs=(hbm, hbm, hbm),
         scratch_shapes=[
+            *[pltpu.VMEM(out.shape, out.dtype) for out in out_shape],
             pltpu.VMEM((n_tok, width), jnp.bfloat16),
+            pltpu.VMEM((n_exp, width), jnp.bfloat16),
+            pltpu.VMEM((1, n_tok), jnp.int32),
+            pltpu.VMEM((1, n_tok), jnp.int32),
+            pltpu.VMEM((1, n_tok), jnp.int32),
             pltpu.VMEM((ff // c1, width, c1), jnp.bfloat16),
             pltpu.VMEM((width // c2, ff, c2), jnp.bfloat16),
             block, block, block, block,
@@ -242,12 +282,12 @@
             pltpu.VMEM((n_tok, width), jnp.float32),
             pltpu.VMEM((n, stat_rows, 128), jnp.float32),
             pltpu.VMEM((n_dp, stat_rows, 128), jnp.float32),
-            dma, dma((ff // c1,)), dma((width // c2,)),
+            dma((5,)), dma((4,)), dma((ff // c1,)), dma((width // c2,)),
             dma((chunks, n)), dma((chunks, n)), dma((chunks, n)), dma((chunks, n)),
             dma((n,)), dma((n,)), dma((n_dp,)), dma((n_dp,)),
         ],
         compiler_params=pltpu.CompilerParams(
-            collective_id=0, has_side_effects=True, vmem_limit_bytes=40 * 2**20
+            collective_id=0, has_side_effects=True, vmem_limit_bytes=VMEM_LIMIT
         ),
         cost_estimate=pl.CostEstimate(
             flops=4 * rows * width * ff, bytes_accessed=4 * width * ff, transcendentals=rows * ff
@@ -256,6 +296,11 @@
         tokens, router.T, w_in, w_out,
         assign.reshape(1, n_tok), modality.reshape(1, n_tok), slot.reshape(1, n_tok),
     )
+    return pl.pallas_call(
+        write_out, out_shape=out_shape, in_specs=[hbm] * 3, out_specs=(hbm,) * 3,
+        scratch_shapes=[dma((3,))],
+        compiler_params=pltpu.CompilerParams(vmem_limit_bytes=VMEM_LIMIT),
+    )(*results)
 
 
 def solution(mesh):

time: 41.9 us -> 48.2 us (1.15)
  Pallas kernels: 30.9 us -> 47.4 us
  local copies, waits for them, and re-layouts: 10.1 us -> 0 us
    pallas_call x0 -> x1, Pallas kernels: none -> 17.1 us  [per_device(): pl.pallas_call(write_out, out_shape=out_shape, in_specs=[hbm] * 3, out_sp...]
    unnamed x17 -> x0, local copies, waits for them, and re-layouts: 10.1 us -> none
    pallas_call x1, Pallas kernels: 30.9 us -> 30.4 us  [per_device(): pl.pallas_call(functools.partial(kernel, n, n_dp, cap, chunks), out_shape...]
where the time goes in v2:
time: 48.2 us; the launch traced here: 48.1 us
  Pallas kernels  47.4 us (98%)
  between operations  0.64 us (1%)
    pallas_call x1, Pallas kernels, per_device(): pl.pallas_call(functools.partial(kernel, n, n_dp, cap, chunks), out_shape...  30.4 us
    pallas_call x1, Pallas kernels, per_device(): pl.pallas_call(write_out, out_shape=out_shape, in_specs=[hbm] * 3, out_sp...  17.1 us

profile of v2, /device:TPU:0, one launch (start us, length us, event | category | flops | bytes accessed | tf_op | source)
XLA Modules:
  0.0 48.1 jit_solution(14040626513970126442)
XLA Ops:
  0.6 30.4 %shard_map.94 = (bf16[256,1024]{1,0:T(8,128)(2,1)}, f32[2,4]{1,0:T(2,128)}, f32[2,2]{1,0:T(2,128)}) custom-call(bf16[256,1024]{1,0:T(8,128)(2,1)} %tokens_hbm.1, bf16[4,1024]{1,0:T(4,128)(2,1)} %bitcast.4, bf16[1,1024,2048]{2,1,0:T(8,128)(2,1)} %w_in_hbm.1, bf16[1,2048,1024]{2,1,0:T(8,128)(2,1)} %w_out_hbm.1, s32[1,256]{1,0:T(1,128)} %bitcast.5, ...), custom_call_target="tpu_custom_call" | custom-call | flops 3221225472 | bytes 8388608 | tf_op jit(solution)/shard_map/pallas_call | solution.py:266
  31.0 17.1 %shard_map.95 = (bf16[256,1024]{1,0:T(8,128)(2,1)}, f32[2,4]{1,0:T(2,128)}, f32[2,2]{1,0:T(2,128)}) custom-call(bf16[256,1024]{1,0:T(8,128)(2,1)} %get-tuple-element.6.refs_0_, f32[2,4]{1,0:T(2,128)} %get-tuple-element.7.refs_1_, f32[2,2]{1,0:T(2,128)} %get-tuple-element.8.refs_2_), custom_call_target="tpu_custom_call" | custom-call | tf_op jit(solution)/shard_map/pallas_call | solution.py:299

commit v3 on v2

--- a/solution.py
+++ b/solution.py
@@ -29,8 +29,8 @@
 def kernel(
     n, n_dp, cap, chunks,
     tokens_hbm, router_hbm, w_in_hbm, w_out_hbm, assign_hbm, modality_hbm, slot_hbm,
-    mixed_hbm, importance_hbm, entropies_hbm,
-    mixed, importance, entropies, tokens, router_t, assign, modality, slot, w1, w2, buf, recv, res, ret, hidden, chosen, stat1, stat2,
+    ret, take_hbm, gates_hbm, importance_hbm, entropies_hbm,
+    take, gates, importance, entropies, tokens, router_t, assign, modality, slot, w1, w2, buf, recv, res, hidden, stat1, stat2,
     in_sem, out_sem, w1_sem, w2_sem, out_send, out_recv, back_send, back_recv, s1_send, s1_recv, s2_send, s2_recv,
 ):
     me = lax.axis_index("expert")
@@ -73,10 +73,10 @@
         rel == 0, where_slot, cap + piece * span + (rel - 1) * part + where_slot - piece * part
     )
 
-    def place(start, count):
+    def place(dst, start, count):
         rows = lax.broadcasted_iota(jnp.int32, (count, n_tok), 0) + start
         one_hot = jnp.where(rows == label, 1.0, 0.0).astype(jnp.bfloat16)
-        buf[start : start + count, :] = jnp.dot(
+        dst[start : start + count, :] = jnp.dot(
             one_hot, tokens[...], preferred_element_type=jnp.float32
         ).astype(jnp.bfloat16)
 
@@ -103,12 +103,12 @@
     for j in range(n2):
         w2_copy(j).start()
     for c in range(chunks):
-        place(cap + c * span, span)
+        place(buf, cap + c * span, span)
         if c == 0:
             pl.semaphore_wait(barrier, n - 1 + n_dp - 1)
         for k in reversed(range(1, n)):
             out_copy(c, k).start()
-    place(0, cap)
+    place(recv, 0, cap)
 
     loads[3].wait()
     loads[4].wait()
@@ -150,50 +150,54 @@
     for k in range(1, n):
         s1_copy(k).start()
 
-    def experts(src, dst, start, count, first):
+    def experts(start, count, first):
         for j in range(n1):
             if first:
                 w1_copy(j).wait()
             act = jax.nn.gelu(
-                jnp.dot(src[start : start + count, :], w1[j], preferred_element_type=jnp.float32)
+                jnp.dot(recv[start : start + count, :], w1[j], preferred_element_type=jnp.float32)
             )
             hidden[0:count, pl.ds(j * c1, c1)] = act.astype(jnp.bfloat16)
-
         for j in range(n2):
             if first:
                 w2_copy(j).wait()
-            dst[start : start + count, pl.ds(j * c2, c2)] = jnp.dot(
+            res[start : start + count, pl.ds(j * c2, c2)] = jnp.dot(
                 hidden[0:count, :], w2[j], preferred_element_type=jnp.float32
             ).astype(jnp.bfloat16)
 
-    experts(buf, ret, 0, cap, True)
-
-    for k in range(1, n):
-        s1_copy(k).wait()
-    stat2[me_dp] = sum(stat1[i] for i in range(n))
-    for k in range(1, n_dp):
-        s2_copy(k).start()
+    wanted = to_columns(label.astype(jnp.float32))[:, 0:1]
+    lanes = lax.broadcasted_iota(jnp.int32, take.shape, 1).astype(jnp.float32)
+    take[...] = jnp.where(lanes == wanted, 1.0, 0.0).astype(jnp.bfloat16)
+    gates[...] = to_columns(gate)
+    stores = [
+        pltpu.make_async_copy(take, take_hbm, out_sem.at[0]),
+        pltpu.make_async_copy(gates, gates_hbm, out_sem.at[1]),
+    ]
+    for store in stores:
+        store.start()
+
+    def first_sums():
+        for k in range(1, n):
+            s1_copy(k).wait()
+        stat2[me_dp] = sum(stat1[i] for i in range(n))
+        for k in range(1, n_dp):
+            s2_copy(k).start()
 
     for c in range(chunks):
         for k in range(1, n):
             out_copy(c, k).wait_recv()
-        experts(recv, res, cap + c * span, span, False)
+        if c == 0:
+            experts(0, cap + span, True)
+        else:
+            experts(cap + c * span, span, False)
         for k in reversed(range(1, n)):
             back_copy(c, k).start()
-
-    label_columns = to_columns(label.astype(jnp.float32))
-    gate_column = to_columns(gate)[:, 0:1]
-
-    def gather(start, count, first=0, length=n_tok):
-        lanes = lax.broadcasted_iota(jnp.int32, (length, count), 1) + start
-        wanted = label_columns[first : first + length, 0:1]
-        one_hot = jnp.where(lanes.astype(jnp.float32) == wanted, 1.0, 0.0)
-        return jnp.dot(
-            one_hot.astype(jnp.bfloat16), ret[start : start + count, :],
-            preferred_element_type=jnp.float32,
-        )
-
-    chosen[...] = gather(0, cap)
+        if c == 0:
+            stores.append(
+                pltpu.make_async_copy(res.at[pl.ds(0, cap)], ret.at[pl.ds(0, cap)], out_sem.at[2])
+            )
+            stores[-1].start()
+            first_sums()
 
     for k in range(1, n_dp):
         s2_copy(k).wait()
@@ -204,46 +208,56 @@
     logs = jnp.log(jnp.where(mean == 0.0, 1.0, mean))
     entropies[:, 0:1] = totals[0:2, n_exp + 1 : n_exp + 2] / denom
     entropies[:, 1:2] = -jnp.sum(mean * logs, axis=1, keepdims=True)
-
-    stores = [
-        pltpu.make_async_copy(importance, importance_hbm, out_sem.at[0]),
-        pltpu.make_async_copy(entropies, entropies_hbm, out_sem.at[1]),
-    ]
-    for store in stores:
+    stores.append(pltpu.make_async_copy(importance, importance_hbm, out_sem.at[3]))
+    stores.append(pltpu.make_async_copy(entropies, entropies_hbm, out_sem.at[4]))
+    for store in stores[-2:]:
         store.start()
 
     for c in range(chunks):
         for k in range(1, n):
-            back_copy(c, k).wait_recv()
-        if c < chunks - 1:
-            chosen[...] += gather(cap + c * span, span)
-    half = n_tok // 2
-    for i in range(2):
-        rows = pl.ds(i * half, half)
-        last = gather(cap + (chunks - 1) * span, span, i * half, half)
-        mixed[rows, :] = (
-            gate_column[i * half : (i + 1) * half] * (chosen[rows, :] + last)
-        ).astype(jnp.bfloat16)
+            out_copy(c, k).wait_send()
+            back_copy(c, k).wait()
+    for store in stores:
+        store.wait()
+
+
+def combine(
+    ret_hbm, take_hbm, gates_hbm, importance_in, entropies_in,
+    mixed_hbm, importance_hbm, entropies_hbm,
+    ret, take, gates, importance, entropies, mixed, in_sem, out_sem,
+):
+    blocks, _, step = ret.shape
+    small = (
+        (take_hbm, take, None), (gates_hbm, gates, None),
+        (importance_in, importance, importance_hbm), (entropies_in, entropies, entropies_hbm),
+    )
+    loads = [pltpu.make_async_copy(a, b, in_sem.at[i]) for i, (a, b, _) in enumerate(small)]
+    columns = [pl.ds(j * step, step) for j in range(blocks)]
+    pieces = [
+        pltpu.make_async_copy(ret_hbm.at[:, columns[j]], ret.at[j], in_sem.at[len(small) + j])
+        for j in range(blocks)
+    ]
+    for load in [*loads[:2], *pieces, *loads[2:]]:
+        load.start()
+    loads[0].wait()
+    loads[1].wait()
+    stores = []
+    for j in range(blocks):
+        pieces[j].wait()
+        rows = jnp.dot(take[...], ret[j], preferred_element_type=jnp.float32)
+        mixed[j] = (gates[:, 0:1] * rows).astype(jnp.bfloat16)
         stores.append(
-            pltpu.make_async_copy(mixed.at[rows], mixed_hbm.at[rows], out_sem.at[2 + i])
+            pltpu.make_async_copy(mixed.at[j], mixed_hbm.at[:, columns[j]], out_sem.at[j])
+        )
+        stores[-1].start()
+    for i in (2, 3):
+        loads[i].wait()
+        stores.append(
+            pltpu.make_async_copy(small[i][1], small[i][2], out_sem.at[blocks + i - 2])
         )
         stores[-1].start()
     for store in stores:
         store.wait()
-
-    for c in range(chunks):
-        for k in range(1, n):
-            out_copy(c, k).wait_send()
-            back_copy(c, k).wait_send()
-
-
-def write_out(*refs):
-    sems, count = refs[-1], (len(refs) - 1) // 2
-    copies = [pltpu.make_async_copy(refs[i], refs[count + i], sems.at[i]) for i in range(count)]
-    for copy in copies:
-        copy.start()
-    for copy in copies:
-        copy.wait()
 
 
 def per_device(n, n_dp, tokens, router, w_in, w_out, assign, modality, slot):
@@ -258,18 +272,22 @@
     hbm = pl.BlockSpec(memory_space=pltpu.HBM)
     dma = pltpu.SemaphoreType.DMA
     block = pltpu.VMEM((rows, width), jnp.bfloat16)
-    out_shape = (
-        jax.ShapeDtypeStruct((n_tok, width), jnp.bfloat16),
-        jax.ShapeDtypeStruct((2, n_exp), jnp.float32),
-        jax.ShapeDtypeStruct((2, 2), jnp.float32),
-    )
+    f32, bf16 = jnp.float32, jnp.bfloat16
+    stats_shape = [jax.ShapeDtypeStruct((2, n_exp), f32), jax.ShapeDtypeStruct((2, 2), f32)]
+    mixed_shape = jax.ShapeDtypeStruct((n_tok, width), bf16)
+    carried = [
+        jax.ShapeDtypeStruct((rows, width), bf16),
+        jax.ShapeDtypeStruct((n_tok, rows), bf16),
+        jax.ShapeDtypeStruct((n_tok, 128), f32),
+        *stats_shape,
+    ]
     results = pl.pallas_call(
         functools.partial(kernel, n, n_dp, cap, chunks),
-        out_shape=out_shape,
+        out_shape=carried,
         in_specs=[hbm] * 7,
-        out_specs=(hbm, hbm, hbm),
+        out_specs=[hbm] * 5,
         scratch_shapes=[
-            *[pltpu.VMEM(out.shape, out.dtype) for out in out_shape],
+            *[pltpu.VMEM(out.shape, out.dtype) for out in carried[1:]],
             pltpu.VMEM((n_tok, width), jnp.bfloat16),
             pltpu.VMEM((n_exp, width), jnp.bfloat16),
             pltpu.VMEM((1, n_tok), jnp.int32),
@@ -277,12 +295,11 @@
             pltpu.VMEM((1, n_tok), jnp.int32),
             pltpu.VMEM((ff // c1, width, c1), jnp.bfloat16),
             pltpu.VMEM((width // c2, ff, c2), jnp.bfloat16),
-            block, block, block, block,
-            pltpu.VMEM((max(cap, rows - cap), ff), jnp.bfloat16),
-            pltpu.VMEM((n_tok, width), jnp.float32),
+            block, block, block,
+            pltpu.VMEM((rows, ff), jnp.bfloat16),
             pltpu.VMEM((n, stat_rows, 128), jnp.float32),
             pltpu.VMEM((n_dp, stat_rows, 128), jnp.float32),
-            dma((5,)), dma((4,)), dma((ff // c1,)), dma((width // c2,)),
+            dma((5,)), dma((5,)), dma((ff // c1,)), dma((width // c2,)),
             dma((chunks, n)), dma((chunks, n)), dma((chunks, n)), dma((chunks, n)),
             dma((n,)), dma((n,)), dma((n_dp,)), dma((n_dp,)),
         ],
@@ -296,9 +313,18 @@
         tokens, router.T, w_in, w_out,
         assign.reshape(1, n_tok), modality.reshape(1, n_tok), slot.reshape(1, n_tok),
     )
+    blocks = width // c2
     return pl.pallas_call(
-        write_out, out_shape=out_shape, in_specs=[hbm] * 3, out_specs=(hbm,) * 3,
-        scratch_shapes=[dma((3,))],
+        combine,
+        out_shape=[mixed_shape, *stats_shape],
+        in_specs=[hbm] * 5,
+        out_specs=[hbm] * 3,
+        scratch_shapes=[
+            pltpu.VMEM((blocks, rows, c2), bf16),
+            *[pltpu.VMEM(out.shape, out.dtype) for out in carried[1:]],
+            pltpu.VMEM((blocks, n_tok, c2), bf16),
+            dma((4 + blocks,)), dma((2 + blocks,)),
+        ],
         compiler_params=pltpu.CompilerParams(vmem_limit_bytes=VMEM_LIMIT),
     )(*results)
 

time: 48.2 us -> 32.6 us (0.68)
  Pallas kernels: 47.4 us -> 31.8 us
    pallas_call x1, Pallas kernels: 17.1 us -> 3.01 us  [per_device(): pl.pallas_call(combine, out_shape=[mixed_shape, *stats_shape], in_specs=[...]
    pallas_call x1, Pallas kernels: 30.4 us -> 28.8 us  [per_device(): pl.pallas_call(functools.partial(kernel, n, n_dp, cap, chunks), out_shape...]
where the time goes in v3:
time: 32.6 us; the launch traced here: 32.4 us
  Pallas kernels  31.8 us (98%)
  between operations  0.64 us (2%)
    pallas_call x1, Pallas kernels, per_device(): pl.pallas_call(functools.partial(kernel, n, n_dp, cap, chunks), out_shape...  28.8 us
    pallas_call x1, Pallas kernels, per_device(): pl.pallas_call(combine, out_shape=[mixed_shape, *stats_shape], in_specs=[...  3.01 us

profile of v3, /device:TPU:0, one launch (start us, length us, event | category | flops | bytes accessed | tf_op | source)
XLA Modules:
  0.0 32.4 jit_solution(5267290020586902847)
XLA Ops:
  0.6 28.8 %shard_map.94 = (bf16[384,1024]{1,0:T(8,128)(2,1)}, bf16[256,384]{1,0:T(8,128)(2,1)}, f32[256,128]{1,0:T(8,128)}, f32[2,4]{1,0:T(2,128)}, f32[2,2]{1,0:T(2,128)}) custom-call(bf16[256,1024]{1,0:T(8,128)(2,1)} %tokens_hbm.1, bf16[4,1024]{1,0:T(4,128)(2,1)} %bitcast.4, bf16[1,1024,2048]{2,1,0:T(8,128)(2,1)} %w_in_hbm.1, bf16[1,2048,1024]{2,1,0:T(8,128)(2,1)} %w_out_hbm.1, ...), custom_call_target="tpu_custom_call" | custom-call | flops 3221225472 | bytes 8388608 | tf_op jit(solution)/shard_map/pallas_call | solution.py:284
  29.4 3.0 %shard_map.95 = (bf16[256,1024]{1,0:T(8,128)(2,1)}, f32[2,4]{1,0:T(2,128)}, f32[2,2]{1,0:T(2,128)}) custom-call(bf16[384,1024]{1,0:T(8,128)(2,1)} %get-tuple-element.8.ret_hbm, bf16[256,384]{1,0:T(8,128)(2,1)} %get-tuple-element.9.take_hbm, f32[256,128]{1,0:T(8,128)} %get-tuple-element.10.gates_hbm, f32[2,4]{1,0:T(2,128)} %get-tuple-element.11.importance_in, ...), custom_call_target="tpu_custom_call" | custom-call | tf_op jit(solution)/shard_map/pallas_call | solution.py:317

commit v4 on v3

--- a/solution.py
+++ b/solution.py
@@ -265,7 +265,7 @@
     n_exp = router.shape[1]
     ff = w_in.shape[2]
     cap = -(-(3 * n_tok // (2 * n_exp)) // 16) * 16
-    chunks = 2 if cap % 32 == 0 else 1
+    chunks = next(c for c in (3, 2, 1) if cap % (16 * c) == 0)
     rows = n * cap
     c1, c2 = min(ff, 512), min(width, 256)
     stat_rows = -(-(n_exp + 2) // 8) * 8

time: 32.6 us -> 30.6 us (0.939)
  Pallas kernels: 31.8 us -> 29.8 us
    pallas_call x1, Pallas kernels: 28.8 us -> 26.8 us  [per_device(): pl.pallas_call(functools.partial(kernel, n, n_dp, cap, chunks), out_shape...]
where the time goes in v4:
time: 30.6 us; the launch traced here: 30.5 us
  Pallas kernels  29.8 us (97%)
  between operations  0.64 us (2%)
    pallas_call x1, Pallas kernels, per_device(): pl.pallas_call(functools.partial(kernel, n, n_dp, cap, chunks), out_shape...  26.8 us
    pallas_call x1, Pallas kernels, per_device(): pl.pallas_call(combine, out_shape=[mixed_shape, *stats_shape], in_specs=[...  3.01 us

profile of v4, /device:TPU:0, one launch (start us, length us, event | category | flops | bytes accessed | tf_op | source)
XLA Modules:
  0.0 30.5 jit_solution(11468021985014030658)
XLA Ops:
  0.6 26.8 %shard_map.94 = (bf16[384,1024]{1,0:T(8,128)(2,1)}, bf16[256,384]{1,0:T(8,128)(2,1)}, f32[256,128]{1,0:T(8,128)}, f32[2,4]{1,0:T(2,128)}, f32[2,2]{1,0:T(2,128)}) custom-call(bf16[256,1024]{1,0:T(8,128)(2,1)} %tokens_hbm.1, bf16[4,1024]{1,0:T(4,128)(2,1)} %bitcast.4, bf16[1,1024,2048]{2,1,0:T(8,128)(2,1)} %w_in_hbm.1, bf16[1,2048,1024]{2,1,0:T(8,128)(2,1)} %w_out_hbm.1, ...), custom_call_target="tpu_custom_call" | custom-call | flops 3221225472 | bytes 8388608 | tf_op jit(solution)/shard_map/pallas_call | solution.py:284
  27.5 3.0 %shard_map.95 = (bf16[256,1024]{1,0:T(8,128)(2,1)}, f32[2,4]{1,0:T(2,128)}, f32[2,2]{1,0:T(2,128)}) custom-call(bf16[384,1024]{1,0:T(8,128)(2,1)} %get-tuple-element.8.ret_hbm, bf16[256,384]{1,0:T(8,128)(2,1)} %get-tuple-element.9.take_hbm, f32[256,128]{1,0:T(8,128)} %get-tuple-element.10.gates_hbm, f32[2,4]{1,0:T(2,128)} %get-tuple-element.11.importance_in, ...), custom_call_target="tpu_custom_call" | custom-call | tf_op jit(solution)/shard_map/pallas_call | solution.py:317

commit v5 on v4

--- a/solution.py
+++ b/solution.py
@@ -1,4 +1,5 @@
 import functools
+import math
 
 import jax
 import jax.numpy as jnp
@@ -22,6 +23,12 @@
     return out
 
 
+def gelu(x):
+    scale = math.sqrt(2.0 / math.pi)
+    half = 0.5 * x
+    return half + half * jnp.tanh(x * (scale + (scale * 0.044715) * (x * x)))
+
+
 def to_columns(row):
     return jnp.transpose(jnp.broadcast_to(row, (128, row.shape[1])))
 
@@ -30,8 +37,9 @@
     n, n_dp, cap, chunks,
     tokens_hbm, router_hbm, w_in_hbm, w_out_hbm, assign_hbm, modality_hbm, slot_hbm,
     ret, take_hbm, gates_hbm, importance_hbm, entropies_hbm,
-    take, gates, importance, entropies, tokens, router_t, assign, modality, slot, w1, w2, buf, recv, res, hidden, stat1, stat2,
+    take, gates, importance, entropies, tokens, router_t, assign, modality, slot, w1, w2, buf, recv, res, hidden, stat1, stat2, stat3,
     in_sem, out_sem, w1_sem, w2_sem, out_send, out_recv, back_send, back_recv, s1_send, s1_recv, s2_send, s2_recv,
+    s3_send, s3_recv, entered,
 ):
     me = lax.axis_index("expert")
     me_dp = lax.axis_index("dp")
@@ -42,6 +50,21 @@
     part = cap // chunks
     span = (n - 1) * part
 
+    barrier = pltpu.get_barrier_semaphore()
+    for k in range(1, n):
+        @pl.when(me != k)
+        def _():
+            pl.semaphore_signal(
+                barrier, inc=1, device_id={"expert": peers[k]}, device_id_type=MESH
+            )
+
+    @pl.when(me == 0)
+    def _():
+        for k in range(1, n_dp):
+            pl.semaphore_signal(
+                barrier, inc=1, device_id={"dp": peers_dp[k]}, device_id_type=MESH
+            )
+
     pairs = (
         (assign_hbm, assign), (slot_hbm, slot), (tokens_hbm, tokens),
         (router_hbm, router_t), (modality_hbm, modality),
@@ -49,11 +72,16 @@
     loads = [pltpu.make_async_copy(a, b, in_sem.at[i]) for i, (a, b) in enumerate(pairs)]
     for load in loads:
         load.start()
-    barrier = pltpu.get_barrier_semaphore()
-    for k in range(1, n):
-        pl.semaphore_signal(barrier, inc=1, device_id={"expert": peers[k]}, device_id_type=MESH)
-    for k in range(1, n_dp):
-        pl.semaphore_signal(barrier, inc=1, device_id={"dp": peers_dp[k]}, device_id_type=MESH)
+
+    def await_group():
+        @pl.when(me != 0)
+        def _():
+            pl.semaphore_wait(barrier, n - 1)
+            pl.semaphore_signal(entered, inc=1, device_id={"expert": 0}, device_id_type=MESH)
+
+        @pl.when(me == 0)
+        def _():
+            pl.semaphore_wait(entered, n - 1)
 
     n1, n2 = w1.shape[0], w2.shape[0]
     c1, c2 = w1.shape[2], w2.shape[2]
@@ -105,7 +133,7 @@
     for c in range(chunks):
         place(buf, cap + c * span, span)
         if c == 0:
-            pl.semaphore_wait(barrier, n - 1 + n_dp - 1)
+            await_group()
         for k in reversed(range(1, n)):
             out_copy(c, k).start()
     place(recv, 0, cap)
@@ -135,10 +163,10 @@
     stat1[me, n_exp : n_exp + 1, :] = by_kind(jnp.ones_like(gate))
     stat1[me, n_exp + 1 : n_exp + 2, :] = by_kind(entropy)
 
-    def s1_copy(k):
+    def s1_copy(i):
         return pltpu.make_async_remote_copy(
-            src_ref=stat1.at[me], dst_ref=stat1.at[me], send_sem=s1_send.at[k],
-            recv_sem=s1_recv.at[k], device_id={"expert": peers[k]}, device_id_type=MESH,
+            src_ref=stat1.at[i], dst_ref=stat1.at[i], send_sem=s1_send,
+            recv_sem=s1_recv.at[i], device_id={"expert": 0}, device_id_type=MESH,
         )
 
     def s2_copy(k):
@@ -147,14 +175,47 @@
             recv_sem=s2_recv.at[k], device_id={"dp": peers_dp[k]}, device_id_type=MESH,
         )
 
-    for k in range(1, n):
-        s1_copy(k).start()
+    def s3_copy(k):
+        return pltpu.make_async_remote_copy(
+            src_ref=stat3, dst_ref=stat3, send_sem=s3_send.at[k], recv_sem=s3_recv,
+            device_id={"expert": k}, device_id_type=MESH,
+        )
+
+    @pl.when(me != 0)
+    def _():
+        s1_copy(me).start()
+
+    def first_sums():
+        @pl.when(me == 0)
+        def _():
+            for i in range(1, n):
+                s1_copy(i).wait_recv()
+            stat2[me_dp] = sum(stat1[i] for i in range(n))
+            pl.semaphore_wait(barrier, n_dp - 1)
+            for k in range(1, n_dp):
+                s2_copy(k).start()
+
+    def last_sums():
+        @pl.when(me == 0)
+        def _():
+            for k in range(1, n_dp):
+                s2_copy(k).wait()
+            stat3[...] = sum(stat2[i] for i in range(n_dp))
+            for k in range(1, n):
+                s3_copy(k).start()
+            for k in range(1, n):
+                s3_copy(k).wait_send()
+
+        @pl.when(me != 0)
+        def _():
+            s1_copy(me).wait_send()
+            s3_copy(0).wait_recv()
 
     def experts(start, count, first):
         for j in range(n1):
             if first:
                 w1_copy(j).wait()
-            act = jax.nn.gelu(
+            act = gelu(
                 jnp.dot(recv[start : start + count, :], w1[j], preferred_element_type=jnp.float32)
             )
             hidden[0:count, pl.ds(j * c1, c1)] = act.astype(jnp.bfloat16)
@@ -175,13 +236,6 @@
     ]
     for store in stores:
         store.start()
-
-    def first_sums():
-        for k in range(1, n):
-            s1_copy(k).wait()
-        stat2[me_dp] = sum(stat1[i] for i in range(n))
-        for k in range(1, n_dp):
-            s2_copy(k).start()
 
     for c in range(chunks):
         for k in range(1, n):
@@ -199,9 +253,8 @@
             stores[-1].start()
             first_sums()
 
-    for k in range(1, n_dp):
-        s2_copy(k).wait()
-    totals = jnp.transpose(sum(stat2[i] for i in range(n_dp)))
+    last_sums()
+    totals = jnp.transpose(stat3[...])
     denom = jnp.maximum(totals[0:2, n_exp : n_exp + 1], 1.0)
     mean = totals[0:2, 0:n_exp] / denom
     importance[...] = mean
@@ -299,9 +352,11 @@
             pltpu.VMEM((rows, ff), jnp.bfloat16),
             pltpu.VMEM((n, stat_rows, 128), jnp.float32),
             pltpu.VMEM((n_dp, stat_rows, 128), jnp.float32),
+            pltpu.VMEM((stat_rows, 128), jnp.float32),
             dma((5,)), dma((5,)), dma((ff // c1,)), dma((width // c2,)),
             dma((chunks, n)), dma((chunks, n)), dma((chunks, n)), dma((chunks, n)),
-            dma((n,)), dma((n,)), dma((n_dp,)), dma((n_dp,)),
+            dma, dma((n,)), dma((n_dp,)), dma((n_dp,)), dma((n,)), dma,
+            pltpu.SemaphoreType.REGULAR,
         ],
         compiler_params=pltpu.CompilerParams(
             collective_id=0, has_side_effects=True, vmem_limit_bytes=VMEM_LIMIT

time: 30.6 us -> 28.3 us (0.925)
  Pallas kernels: 29.8 us -> 27.5 us
    pallas_call x1, Pallas kernels: 26.8 us -> 24.5 us  [per_device(): pl.pallas_call(functools.partial(kernel, n, n_dp, cap, chunks), out_shape...]
where the time goes in v5:
time: 28.3 us; the launch traced here: 28.1 us
  Pallas kernels  27.5 us (97%)
  between operations  0.64 us (2%)
    pallas_call x1, Pallas kernels, per_device(): pl.pallas_call(functools.partial(kernel, n, n_dp, cap, chunks), out_shape...  24.5 us
    pallas_call x1, Pallas kernels, per_device(): pl.pallas_call(combine, out_shape=[mixed_shape, *stats_shape], in_specs=[...  3.01 us

profile of v5, /device:TPU:0, one launch (start us, length us, event | category | flops | bytes accessed | tf_op | source)
XLA Modules:
  0.0 28.1 jit_solution(14831758104952654973)
XLA Ops:
  0.6 24.5 %shard_map.94 = (bf16[384,1024]{1,0:T(8,128)(2,1)}, bf16[256,384]{1,0:T(8,128)(2,1)}, f32[256,128]{1,0:T(8,128)}, f32[2,4]{1,0:T(2,128)}, f32[2,2]{1,0:T(2,128)}) custom-call(bf16[256,1024]{1,0:T(8,128)(2,1)} %tokens_hbm.1, bf16[4,1024]{1,0:T(4,128)(2,1)} %bitcast.4, bf16[1,1024,2048]{2,1,0:T(8,128)(2,1)} %w_in_hbm.1, bf16[1,2048,1024]{2,1,0:T(8,128)(2,1)} %w_out_hbm.1, ...), custom_call_target="tpu_custom_call" | custom-call | flops 3221225472 | bytes 8388608 | tf_op jit(solution)/shard_map/pallas_call | solution.py:337
  25.1 3.0 %shard_map.95 = (bf16[256,1024]{1,0:T(8,128)(2,1)}, f32[2,4]{1,0:T(2,128)}, f32[2,2]{1,0:T(2,128)}) custom-call(bf16[384,1024]{1,0:T(8,128)(2,1)} %get-tuple-element.8.ret_hbm, bf16[256,384]{1,0:T(8,128)(2,1)} %get-tuple-element.9.take_hbm, f32[256,128]{1,0:T(8,128)} %get-tuple-element.10.gates_hbm, f32[2,4]{1,0:T(2,128)} %get-tuple-element.11.importance_in, ...), custom_call_target="tpu_custom_call" | custom-call | tf_op jit(solution)/shard_map/pallas_call | solution.py:372

commit v6 on v5

--- a/solution.py
+++ b/solution.py
@@ -36,13 +36,15 @@
 def kernel(
     n, n_dp, cap, chunks,
     tokens_hbm, router_hbm, w_in_hbm, w_out_hbm, assign_hbm, modality_hbm, slot_hbm,
-    ret, take_hbm, gates_hbm, importance_hbm, entropies_hbm,
-    take, gates, importance, entropies, tokens, router_t, assign, modality, slot, w1, w2, buf, recv, res, hidden, stat1, stat2, stat3,
+    ret, picks_hbm, importance_hbm, entropies_hbm,
+    picks, importance, entropies, tokens, router_t, assign, modality, slot, w1, w2, buf, recv, res, hidden, stat1, stat2, stat3,
     in_sem, out_sem, w1_sem, w2_sem, out_send, out_recv, back_send, back_recv, s1_send, s1_recv, s2_send, s2_recv,
     s3_send, s3_recv, entered,
 ):
     me = lax.axis_index("expert")
     me_dp = lax.axis_index("dp")
+    lead = n - 1
+    others = range(n - 1)
     peers = [partner(me, k, n) for k in range(n)]
     peers_dp = [partner(me_dp, k, n_dp) for k in range(n_dp)]
     n_tok, width = tokens.shape
@@ -52,13 +54,13 @@
 
     barrier = pltpu.get_barrier_semaphore()
     for k in range(1, n):
-        @pl.when(me != k)
+        @pl.when(me != lead ^ k)
         def _():
             pl.semaphore_signal(
                 barrier, inc=1, device_id={"expert": peers[k]}, device_id_type=MESH
             )
 
-    @pl.when(me == 0)
+    @pl.when(me == lead)
     def _():
         for k in range(1, n_dp):
             pl.semaphore_signal(
@@ -74,12 +76,12 @@
         load.start()
 
     def await_group():
-        @pl.when(me != 0)
+        @pl.when(me != lead)
         def _():
             pl.semaphore_wait(barrier, n - 1)
-            pl.semaphore_signal(entered, inc=1, device_id={"expert": 0}, device_id_type=MESH)
-
-        @pl.when(me == 0)
+            pl.semaphore_signal(entered, inc=1, device_id={"expert": lead}, device_id_type=MESH)
+
+        @pl.when(me == lead)
         def _():
             pl.semaphore_wait(entered, n - 1)
 
@@ -166,7 +168,7 @@
     def s1_copy(i):
         return pltpu.make_async_remote_copy(
             src_ref=stat1.at[i], dst_ref=stat1.at[i], send_sem=s1_send,
-            recv_sem=s1_recv.at[i], device_id={"expert": 0}, device_id_type=MESH,
+            recv_sem=s1_recv.at[i], device_id={"expert": lead}, device_id_type=MESH,
         )
 
     def s2_copy(k):
@@ -181,14 +183,14 @@
             device_id={"expert": k}, device_id_type=MESH,
         )
 
-    @pl.when(me != 0)
+    @pl.when(me != lead)
     def _():
         s1_copy(me).start()
 
     def first_sums():
-        @pl.when(me == 0)
-        def _():
-            for i in range(1, n):
+        @pl.when(me == lead)
+        def _():
+            for i in others:
                 s1_copy(i).wait_recv()
             stat2[me_dp] = sum(stat1[i] for i in range(n))
             pl.semaphore_wait(barrier, n_dp - 1)
@@ -196,17 +198,17 @@
                 s2_copy(k).start()
 
     def last_sums():
-        @pl.when(me == 0)
+        @pl.when(me == lead)
         def _():
             for k in range(1, n_dp):
                 s2_copy(k).wait()
             stat3[...] = sum(stat2[i] for i in range(n_dp))
-            for k in range(1, n):
+            for k in others:
                 s3_copy(k).start()
-            for k in range(1, n):
+            for k in others:
                 s3_copy(k).wait_send()
 
-        @pl.when(me != 0)
+        @pl.when(me != lead)
         def _():
             s1_copy(me).wait_send()
             s3_copy(0).wait_recv()
@@ -226,14 +228,9 @@
                 hidden[0:count, :], w2[j], preferred_element_type=jnp.float32
             ).astype(jnp.bfloat16)
 
-    wanted = to_columns(label.astype(jnp.float32))[:, 0:1]
-    lanes = lax.broadcasted_iota(jnp.int32, take.shape, 1).astype(jnp.float32)
-    take[...] = jnp.where(lanes == wanted, 1.0, 0.0).astype(jnp.bfloat16)
-    gates[...] = to_columns(gate)
-    stores = [
-        pltpu.make_async_copy(take, take_hbm, out_sem.at[0]),
-        pltpu.make_async_copy(gates, gates_hbm, out_sem.at[1]),
-    ]
+    lanes = lax.broadcasted_iota(jnp.int32, picks.shape, 1)
+    picks[...] = jnp.where(lanes == 0, to_columns(label.astype(jnp.float32)), to_columns(gate))
+    stores = [pltpu.make_async_copy(picks, picks_hbm, out_sem.at[0])]
     for store in stores:
         store.start()
 
@@ -248,7 +245,7 @@
             back_copy(c, k).start()
         if c == 0:
             stores.append(
-                pltpu.make_async_copy(res.at[pl.ds(0, cap)], ret.at[pl.ds(0, cap)], out_sem.at[2])
+                pltpu.make_async_copy(res.at[pl.ds(0, cap)], ret.at[pl.ds(0, cap)], out_sem.at[1])
             )
             stores[-1].start()
             first_sums()
@@ -261,8 +258,8 @@
     logs = jnp.log(jnp.where(mean == 0.0, 1.0, mean))
     entropies[:, 0:1] = totals[0:2, n_exp + 1 : n_exp + 2] / denom
     entropies[:, 1:2] = -jnp.sum(mean * logs, axis=1, keepdims=True)
-    stores.append(pltpu.make_async_copy(importance, importance_hbm, out_sem.at[3]))
-    stores.append(pltpu.make_async_copy(entropies, entropies_hbm, out_sem.at[4]))
+    stores.append(pltpu.make_async_copy(importance, importance_hbm, out_sem.at[2]))
+    stores.append(pltpu.make_async_copy(entropies, entropies_hbm, out_sem.at[3]))
     for store in stores[-2:]:
         store.start()
 
@@ -275,40 +272,34 @@
 
 
 def combine(
-    ret_hbm, take_hbm, gates_hbm, importance_in, entropies_in,
-    mixed_hbm, importance_hbm, entropies_hbm,
-    ret, take, gates, importance, entropies, mixed, in_sem, out_sem,
+    ret_hbm, picks_hbm, importance_in, entropies_in, mixed_hbm, importance_hbm, entropies_hbm,
+    ret, picks, importance, entropies, mixed, in_sem, out_sem,
 ):
-    blocks, _, step = ret.shape
-    small = (
-        (take_hbm, take, None), (gates_hbm, gates, None),
-        (importance_in, importance, importance_hbm), (entropies_in, entropies, entropies_hbm),
-    )
-    loads = [pltpu.make_async_copy(a, b, in_sem.at[i]) for i, (a, b, _) in enumerate(small)]
+    blocks, n_rows, step = ret.shape
     columns = [pl.ds(j * step, step) for j in range(blocks)]
-    pieces = [
-        pltpu.make_async_copy(ret_hbm.at[:, columns[j]], ret.at[j], in_sem.at[len(small) + j])
-        for j in range(blocks)
-    ]
-    for load in [*loads[:2], *pieces, *loads[2:]]:
+    pairs = (
+        (picks_hbm, picks), (importance_in, importance), (entropies_in, entropies),
+        *((ret_hbm.at[:, columns[j]], ret.at[j]) for j in range(blocks)),
+    )
+    loads = [pltpu.make_async_copy(a, b, in_sem.at[i]) for i, (a, b) in enumerate(pairs)]
+    pairs = (
+        (importance, importance_hbm), (entropies, entropies_hbm),
+        *((mixed.at[j], mixed_hbm.at[:, columns[j]]) for j in range(blocks)),
+    )
+    stores = [pltpu.make_async_copy(a, b, out_sem.at[i]) for i, (a, b) in enumerate(pairs)]
+    for load in loads:
         load.start()
-    loads[0].wait()
-    loads[1].wait()
-    stores = []
+    for i in range(3):
+        loads[i].wait()
+    for i in range(2):
+        stores[i].start()
+    lanes = lax.broadcasted_iota(jnp.int32, (picks.shape[0], n_rows), 1).astype(jnp.float32)
+    take = jnp.where(lanes == picks[:, 0:1], 1.0, 0.0).astype(jnp.bfloat16)
     for j in range(blocks):
-        pieces[j].wait()
-        rows = jnp.dot(take[...], ret[j], preferred_element_type=jnp.float32)
-        mixed[j] = (gates[:, 0:1] * rows).astype(jnp.bfloat16)
-        stores.append(
-            pltpu.make_async_copy(mixed.at[j], mixed_hbm.at[:, columns[j]], out_sem.at[j])
-        )
-        stores[-1].start()
-    for i in (2, 3):
-        loads[i].wait()
-        stores.append(
-            pltpu.make_async_copy(small[i][1], small[i][2], out_sem.at[blocks + i - 2])
-        )
-        stores[-1].start()
+        loads[3 + j].wait()
+        rows = jnp.dot(take, ret[j], preferred_element_type=jnp.float32)
+        mixed[j] = (picks[:, 1:2] * rows).astype(jnp.bfloat16)
+        stores[2 + j].start()
     for store in stores:
         store.wait()
 
@@ -320,7 +311,7 @@
     cap = -(-(3 * n_tok // (2 * n_exp)) // 16) * 16
     chunks = next(c for c in (3, 2, 1) if cap % (16 * c) == 0)
     rows = n * cap
-    c1, c2 = min(ff, 512), min(width, 256)
+    c1, c2 = min(ff, 256), min(width, 256)
     stat_rows = -(-(n_exp + 2) // 8) * 8
     hbm = pl.BlockSpec(memory_space=pltpu.HBM)
     dma = pltpu.SemaphoreType.DMA
@@ -330,7 +321,6 @@
     mixed_shape = jax.ShapeDtypeStruct((n_tok, width), bf16)
     carried = [
         jax.ShapeDtypeStruct((rows, width), bf16),
-        jax.ShapeDtypeStruct((n_tok, rows), bf16),
         jax.ShapeDtypeStruct((n_tok, 128), f32),
         *stats_shape,
     ]
@@ -338,7 +328,7 @@
         functools.partial(kernel, n, n_dp, cap, chunks),
         out_shape=carried,
         in_specs=[hbm] * 7,
-        out_specs=[hbm] * 5,
+        out_specs=[hbm] * 4,
         scratch_shapes=[
             *[pltpu.VMEM(out.shape, out.dtype) for out in carried[1:]],
             pltpu.VMEM((n_tok, width), jnp.bfloat16),
@@ -353,7 +343,7 @@
             pltpu.VMEM((n, stat_rows, 128), jnp.float32),
             pltpu.VMEM((n_dp, stat_rows, 128), jnp.float32),
             pltpu.VMEM((stat_rows, 128), jnp.float32),
-            dma((5,)), dma((5,)), dma((ff // c1,)), dma((width // c2,)),
+            dma((5,)), dma((4,)), dma((ff // c1,)), dma((width // c2,)),
             dma((chunks, n)), dma((chunks, n)), dma((chunks, n)), dma((chunks, n)),
             dma, dma((n,)), dma((n_dp,)), dma((n_dp,)), dma((n,)), dma,
             pltpu.SemaphoreType.REGULAR,
@@ -372,13 +362,13 @@
     return pl.pallas_call(
         combine,
         out_shape=[mixed_shape, *stats_shape],
-        in_specs=[hbm] * 5,
+        in_specs=[hbm] * 4,
         out_specs=[hbm] * 3,
         scratch_shapes=[
             pltpu.VMEM((blocks, rows, c2), bf16),
             *[pltpu.VMEM(out.shape, out.dtype) for out in carried[1:]],
             pltpu.VMEM((blocks, n_tok, c2), bf16),
-            dma((4 + blocks,)), dma((2 + blocks,)),
+            dma((3 + blocks,)), dma((2 + blocks,)),
         ],
         compiler_params=pltpu.CompilerParams(vmem_limit_bytes=VMEM_LIMIT),
     )(*results)

time: 28.3 us -> 29.8 us (1.053)
  Pallas kernels: 27.5 us -> 29 us
    pallas_call x1, Pallas kernels: 24.5 us -> 26.1 us  [per_device(): pl.pallas_call(functools.partial(kernel, n, n_dp, cap, chunks), out_shape...]
where the time goes in v6:
time: 29.8 us; the launch traced here: 29.6 us
  Pallas kernels  29 us (97%)
  between operations  0.64 us (2%)
    pallas_call x1, Pallas kernels, per_device(): pl.pallas_call(functools.partial(kernel, n, n_dp, cap, chunks), out_shape...  26.1 us
    pallas_call x1, Pallas kernels, per_device(): pl.pallas_call(combine, out_shape=[mixed_shape, *stats_shape], in_specs=[...  2.93 us

profile of v6, /device:TPU:0, one launch (start us, length us, event | category | flops | bytes accessed | tf_op | source)
XLA Modules:
  0.0 29.6 jit_solution(2560726929543237434)
XLA Ops:
  0.6 26.1 %shard_map.94 = (bf16[384,1024]{1,0:T(8,128)(2,1)}, f32[256,128]{1,0:T(8,128)}, f32[2,4]{1,0:T(2,128)}, f32[2,2]{1,0:T(2,128)}) custom-call(bf16[256,1024]{1,0:T(8,128)(2,1)} %tokens_hbm.1, bf16[4,1024]{1,0:T(4,128)(2,1)} %bitcast.4, bf16[1,1024,2048]{2,1,0:T(8,128)(2,1)} %w_in_hbm.1, bf16[1,2048,1024]{2,1,0:T(8,128)(2,1)} %w_out_hbm.1, s32[1,256]{1,0:T(1,128)} %bitcast.5, ...), custom_call_target="tpu_custom_call" | custom-call | flops 3221225472 | bytes 8388608 | tf_op jit(solution)/shard_map/pallas_call | solution.py:327
  26.7 2.9 %shard_map.95 = (bf16[256,1024]{1,0:T(8,128)(2,1)}, f32[2,4]{1,0:T(2,128)}, f32[2,2]{1,0:T(2,128)}) custom-call(bf16[384,1024]{1,0:T(8,128)(2,1)} %get-tuple-element.7.ret_hbm, f32[256,128]{1,0:T(8,128)} %get-tuple-element.8.picks_hbm, f32[2,4]{1,0:T(2,128)} %get-tuple-element.9.importance_in, f32[2,2]{1,0:T(2,128)} %get-tuple-element.10.entropies_in), custom_call_target="tpu_custom_call" | custom-call | tf_op jit(solution)/shard_map/pallas_call | solution.py:362

commit v7 on v6

--- a/solution.py
+++ b/solution.py
@@ -34,7 +34,7 @@
 
 
 def kernel(
-    n, n_dp, cap, chunks,
+    n, n_dp, cap, parts,
     tokens_hbm, router_hbm, w_in_hbm, w_out_hbm, assign_hbm, modality_hbm, slot_hbm,
     ret, picks_hbm, importance_hbm, entropies_hbm,
     picks, importance, entropies, tokens, router_t, assign, modality, slot, w1, w2, buf, recv, res, hidden, stat1, stat2, stat3,
@@ -43,14 +43,16 @@
 ):
     me = lax.axis_index("expert")
     me_dp = lax.axis_index("dp")
-    lead = n - 1
-    others = range(n - 1)
+    lead = 0
+    others = range(1, n)
     peers = [partner(me, k, n) for k in range(n)]
     peers_dp = [partner(me_dp, k, n_dp) for k in range(n_dp)]
     n_tok, width = tokens.shape
     n_exp = router_t.shape[0]
-    part = cap // chunks
-    span = (n - 1) * part
+    starts = [sum(parts[:c]) for c in range(len(parts))]
+    bases = [cap + (n - 1) * start for start in starts]
+    spans = [(n - 1) * part for part in parts]
+    chunks = len(parts)
 
     barrier = pltpu.get_barrier_semaphore()
     for k in range(1, n):
@@ -75,15 +77,18 @@
     for load in loads:
         load.start()
 
-    def await_group():
+    def greet_group():
         @pl.when(me != lead)
         def _():
             pl.semaphore_wait(barrier, n - 1)
-            pl.semaphore_signal(entered, inc=1, device_id={"expert": lead}, device_id_type=MESH)
-
+            pl.semaphore_signal(
+                entered.at[me], inc=1, device_id={"expert": lead}, device_id_type=MESH
+            )
+
+    def await_member(k):
         @pl.when(me == lead)
         def _():
-            pl.semaphore_wait(entered, n - 1)
+            pl.semaphore_wait(entered.at[k], 1)
 
     n1, n2 = w1.shape[0], w2.shape[0]
     c1, c2 = w1.shape[2], w2.shape[2]
@@ -98,10 +103,10 @@
     loads[1].wait()
     rel = jnp.bitwise_xor(assign[...], me)
     where_slot = slot[...]
-    piece = lax.div(where_slot, part)
-    label = jnp.where(
-        rel == 0, where_slot, cap + piece * span + (rel - 1) * part + where_slot - piece * part
-    )
+    label = where_slot
+    for start, base, part in zip(starts, bases, parts):
+        inside = jnp.logical_and(rel > 0, where_slot >= start)
+        label = jnp.where(inside, base + (rel - 1) * part + where_slot - start, label)
 
     def place(dst, start, count):
         rows = lax.broadcasted_iota(jnp.int32, (count, n_tok), 0) + start
@@ -111,7 +116,7 @@
         ).astype(jnp.bfloat16)
 
     def rows_of(c, k):
-        return pl.ds(cap + c * span + (k - 1) * part, part)
+        return pl.ds(bases[c] + (k - 1) * parts[c], parts[c])
 
     def send(src, dst, sems, c, k):
         rows = rows_of(c, k)
@@ -133,10 +138,12 @@
     for j in range(n2):
         w2_copy(j).start()
     for c in range(chunks):
-        place(buf, cap + c * span, span)
+        place(buf, bases[c], spans[c])
         if c == 0:
-            await_group()
+            greet_group()
         for k in reversed(range(1, n)):
+            if c == 0:
+                await_member(k)
             out_copy(c, k).start()
     place(recv, 0, cap)
 
@@ -238,9 +245,9 @@
         for k in range(1, n):
             out_copy(c, k).wait_recv()
         if c == 0:
-            experts(0, cap + span, True)
+            experts(0, cap + spans[c], True)
         else:
-            experts(cap + c * span, span, False)
+            experts(bases[c], spans[c], False)
         for k in reversed(range(1, n)):
             back_copy(c, k).start()
         if c == 0:
@@ -309,9 +316,11 @@
     n_exp = router.shape[1]
     ff = w_in.shape[2]
     cap = -(-(3 * n_tok // (2 * n_exp)) // 16) * 16
-    chunks = next(c for c in (3, 2, 1) if cap % (16 * c) == 0)
+    units = cap // 16
+    parts = [16 * size for size in (1, units - 1 - units // 3, units // 3) if size]
+    chunks = len(parts)
     rows = n * cap
-    c1, c2 = min(ff, 256), min(width, 256)
+    c1, c2 = min(ff, 512), min(width, 256)
     stat_rows = -(-(n_exp + 2) // 8) * 8
     hbm = pl.BlockSpec(memory_space=pltpu.HBM)
     dma = pltpu.SemaphoreType.DMA
@@ -325,7 +334,7 @@
         *stats_shape,
     ]
     results = pl.pallas_call(
-        functools.partial(kernel, n, n_dp, cap, chunks),
+        functools.partial(kernel, n, n_dp, cap, parts),
         out_shape=carried,
         in_specs=[hbm] * 7,
         out_specs=[hbm] * 4,
@@ -346,7 +355,7 @@
             dma((5,)), dma((4,)), dma((ff // c1,)), dma((width // c2,)),
             dma((chunks, n)), dma((chunks, n)), dma((chunks, n)), dma((chunks, n)),
             dma, dma((n,)), dma((n_dp,)), dma((n_dp,)), dma((n,)), dma,
-            pltpu.SemaphoreType.REGULAR,
+            pltpu.SemaphoreType.REGULAR((n,)),
         ],
         compiler_params=pltpu.CompilerParams(
             collective_id=0, has_side_effects=True, vmem_limit_bytes=VMEM_LIMIT

time: 29.8 us -> 28.4 us (0.953)
  Pallas kernels: 29 us -> 27.6 us
    pallas_call x1, Pallas kernels: 26.1 us -> 24.7 us  [per_device(): pl.pallas_call(functools.partial(kernel, n, n_dp, cap, parts), out_shape=...]
where the time goes in v7:
time: 28.4 us; the launch traced here: 28.3 us
  Pallas kernels  27.6 us (97%)
  between operations  0.64 us (2%)
    pallas_call x1, Pallas kernels, per_device(): pl.pallas_call(functools.partial(kernel, n, n_dp, cap, parts), out_shape=...  24.7 us
    pallas_call x1, Pallas kernels, per_device(): pl.pallas_call(combine, out_shape=[mixed_shape, *stats_shape], in_specs=[...  2.93 us

profile of v7, /device:TPU:0, one launch (start us, length us, event | category | flops | bytes accessed | tf_op | source)
XLA Modules:
  0.0 28.3 jit_solution(11526080156144825768)
XLA Ops:
  0.6 24.7 %shard_map.94 = (bf16[384,1024]{1,0:T(8,128)(2,1)}, f32[256,128]{1,0:T(8,128)}, f32[2,4]{1,0:T(2,128)}, f32[2,2]{1,0:T(2,128)}) custom-call(bf16[256,1024]{1,0:T(8,128)(2,1)} %tokens_hbm.1, bf16[4,1024]{1,0:T(4,128)(2,1)} %bitcast.4, bf16[1,1024,2048]{2,1,0:T(8,128)(2,1)} %w_in_hbm.1, bf16[1,2048,1024]{2,1,0:T(8,128)(2,1)} %w_out_hbm.1, s32[1,256]{1,0:T(1,128)} %bitcast.5, ...), custom_call_target="tpu_custom_call" | custom-call | flops 3221225472 | bytes 8388608 | tf_op jit(solution)/shard_map/pallas_call | solution.py:336
  25.3 2.9 %shard_map.95 = (bf16[256,1024]{1,0:T(8,128)(2,1)}, f32[2,4]{1,0:T(2,128)}, f32[2,2]{1,0:T(2,128)}) custom-call(bf16[384,1024]{1,0:T(8,128)(2,1)} %get-tuple-element.7.ret_hbm, f32[256,128]{1,0:T(8,128)} %get-tuple-element.8.picks_hbm, f32[2,4]{1,0:T(2,128)} %get-tuple-element.9.importance_in, f32[2,2]{1,0:T(2,128)} %get-tuple-element.10.entropies_in), custom_call_target="tpu_custom_call" | custom-call | tf_op jit(solution)/shard_map/pallas_call | solution.py:371

commit v8 on v7

--- a/solution.py
+++ b/solution.py
@@ -132,6 +132,15 @@
     def back_copy(c, k):
         return send(res, ret, (back_send, back_recv), c, k)
 
+    orders = ([n - 1, *range(1, n - 1)], list(reversed(range(1, n))))
+
+    def start_all(copy, c):
+        for parity, order in enumerate(orders):
+            @pl.when(lax.rem(me_dp, 2) == parity)
+            def _():
+                for k in order:
+                    copy(c, k).start()
+
     loads[2].wait()
     for j in range(n1):
         w1_copy(j).start()
@@ -141,10 +150,9 @@
         place(buf, bases[c], spans[c])
         if c == 0:
             greet_group()
-        for k in reversed(range(1, n)):
-            if c == 0:
+            for k in reversed(range(1, n)):
                 await_member(k)
-            out_copy(c, k).start()
+        start_all(out_copy, c)
     place(recv, 0, cap)
 
     loads[3].wait()
@@ -248,8 +256,7 @@
             experts(0, cap + spans[c], True)
         else:
             experts(bases[c], spans[c], False)
-        for k in reversed(range(1, n)):
-            back_copy(c, k).start()
+        start_all(back_copy, c)
         if c == 0:
             stores.append(
                 pltpu.make_async_copy(res.at[pl.ds(0, cap)], ret.at[pl.ds(0, cap)], out_sem.at[1])

time: 28.4 us -> 28.5 us (level)
  no operation moved by 1% of the time
where the time goes in v8:
time: 28.5 us; the launch traced here: 28.3 us
  Pallas kernels  27.7 us (97%)
  between operations  0.64 us (2%)
    pallas_call x1, Pallas kernels, per_device(): pl.pallas_call(functools.partial(kernel, n, n_dp, cap, parts), out_shape=...  24.8 us
    pallas_call x1, Pallas kernels, per_device(): pl.pallas_call(combine, out_shape=[mixed_shape, *stats_shape], in_specs=[...  2.92 us

profile of v8, /device:TPU:0, one launch (start us, length us, event | category | flops | bytes accessed | tf_op | source)
XLA Modules:
  0.0 28.3 jit_solution(343759482423830527)
XLA Ops:
  0.6 24.8 %shard_map.94 = (bf16[384,1024]{1,0:T(8,128)(2,1)}, f32[256,128]{1,0:T(8,128)}, f32[2,4]{1,0:T(2,128)}, f32[2,2]{1,0:T(2,128)}) custom-call(bf16[256,1024]{1,0:T(8,128)(2,1)} %tokens_hbm.1, bf16[4,1024]{1,0:T(4,128)(2,1)} %bitcast.4, bf16[1,1024,2048]{2,1,0:T(8,128)(2,1)} %w_in_hbm.1, bf16[1,2048,1024]{2,1,0:T(8,128)(2,1)} %w_out_hbm.1, s32[1,256]{1,0:T(1,128)} %bitcast.5, ...), custom_call_target="tpu_custom_call" | custom-call | flops 3221225472 | bytes 8388608 | tf_op jit(solution)/shard_map/pallas_call | solution.py:343
  25.4 2.9 %shard_map.95 = (bf16[256,1024]{1,0:T(8,128)(2,1)}, f32[2,4]{1,0:T(2,128)}, f32[2,2]{1,0:T(2,128)}) custom-call(bf16[384,1024]{1,0:T(8,128)(2,1)} %get-tuple-element.7.ret_hbm, f32[256,128]{1,0:T(8,128)} %get-tuple-element.8.picks_hbm, f32[2,4]{1,0:T(2,128)} %get-tuple-element.9.importance_in, f32[2,2]{1,0:T(2,128)} %get-tuple-element.10.entropies_in), custom_call_target="tpu_custom_call" | custom-call | tf_op jit(solution)/shard_map/pallas_call | solution.py:378

commit v9 on v7

--- a/solution.py
+++ b/solution.py
@@ -90,6 +90,7 @@
         def _():
             pl.semaphore_wait(entered.at[k], 1)
 
+    greet_group()
     n1, n2 = w1.shape[0], w2.shape[0]
     c1, c2 = w1.shape[2], w2.shape[2]
 
@@ -139,8 +140,6 @@
         w2_copy(j).start()
     for c in range(chunks):
         place(buf, bases[c], spans[c])
-        if c == 0:
-            greet_group()
         for k in reversed(range(1, n)):
             if c == 0:
                 await_member(k)

time: 28.4 us -> 28.4 us (level)
  no operation moved by 1% of the time
where the time goes in v9:
time: 28.4 us; the launch traced here: 28.3 us
  Pallas kernels  27.6 us (97%)
  between operations  0.64 us (2%)
    pallas_call x1, Pallas kernels, per_device(): pl.pallas_call(functools.partial(kernel, n, n_dp, cap, parts), out_shape=...  24.7 us
    pallas_call x1, Pallas kernels, per_device(): pl.pallas_call(combine, out_shape=[mixed_shape, *stats_shape], in_specs=[...  2.93 us

profile of v9, /device:TPU:0, one launch (start us, length us, event | category | flops | bytes accessed | tf_op | source)
XLA Modules:
  0.0 28.3 jit_solution(11879909753508733227)
XLA Ops:
  0.6 24.7 %shard_map.94 = (bf16[384,1024]{1,0:T(8,128)(2,1)}, f32[256,128]{1,0:T(8,128)}, f32[2,4]{1,0:T(2,128)}, f32[2,2]{1,0:T(2,128)}) custom-call(bf16[256,1024]{1,0:T(8,128)(2,1)} %tokens_hbm.1, bf16[4,1024]{1,0:T(4,128)(2,1)} %bitcast.4, bf16[1,1024,2048]{2,1,0:T(8,128)(2,1)} %w_in_hbm.1, bf16[1,2048,1024]{2,1,0:T(8,128)(2,1)} %w_out_hbm.1, s32[1,256]{1,0:T(1,128)} %bitcast.5, ...), custom_call_target="tpu_custom_call" | custom-call | flops 3221225472 | bytes 8388608 | tf_op jit(solution)/shard_map/pallas_call | solution.py:335
  25.3 2.9 %shard_map.95 = (bf16[256,1024]{1,0:T(8,128)(2,1)}, f32[2,4]{1,0:T(2,128)}, f32[2,2]{1,0:T(2,128)}) custom-call(bf16[384,1024]{1,0:T(8,128)(2,1)} %get-tuple-element.7.ret_hbm, f32[256,128]{1,0:T(8,128)} %get-tuple-element.8.picks_hbm, f32[2,4]{1,0:T(2,128)} %get-tuple-element.9.importance_in, f32[2,2]{1,0:T(2,128)} %get-tuple-element.10.entropies_in), custom_call_target="tpu_custom_call" | custom-call | tf_op jit(solution)/shard_map/pallas_call | solution.py:370
